TPU v7x, 128 devices: a whole 4x4x4 slice. The times are simulated.
128 devices in a mesh: row: 8 (over z_hi, y), col: 16 (over x, z_lo, core).
Axes of the slice: x: 4, y: 4, z: 4 (z_hi: 2, z_lo: 2; z = z_hi * 2 + z_lo), core: 2. Of those that a mesh axis runs over, the one named last changes fastest.
Arguments:
- start_block: float32 [64, 65536], P(None, 'row'), may hold values from -6 to 6
- tile_values: bfloat16 [8, 16, 128, 256, 256], P('row', 'col'), may hold values from -0.03125 to 0.03125
- tile_rows: int32 [8, 16, 128], P('row', 'col'), may hold values from 0 to 31
- tile_cols: int32 [8, 16, 128], P('row', 'col'), may hold values from 0 to 15
Outputs:
- alphas: float32 [3, 64, 64], replicated
- betas: float32 [3, 64, 64], replicated
- final_basis: float32 [64, 65536], P(None, 'row')
All inputs are finite; a program needn't handle non-finite values.
Results may differ from a plain program's by a relative error of at most 0.007.
Values may be sent and summed in bfloat16 or wider, within the bound.
A program may use at most 128 MiB of HBM per device.

v0:
```python
import math

import jax
import jax.numpy as jnp
from jax import lax
from jax.sharding import PartitionSpec as P

ITERS = 3


HIGH = lax.Precision.HIGHEST


def from_root(value, axis, source):
    kept = jnp.where(lax.axis_index(axis) == source, value, 0).astype(value.dtype)
    return lax.psum(kept, axis)


def shards(start_block, tile_values, tile_rows, tile_cols):
    row_count = lax.axis_size("row")
    col_count = lax.axis_size("col")
    row_index = lax.axis_index("row")
    col_index = lax.axis_index("col")
    tiles_here = tile_values[0, 0]
    rows_here = tile_rows[0, 0]
    cols_here = tile_cols[0, 0]
    tile_width = tiles_here.shape[1]
    vectors, cell_rows = start_block.shape
    cell_cols = cell_rows * row_count // col_count
    row_blocks = cell_rows // tile_width
    col_blocks = cell_cols // tile_width
    total_rows = cell_rows * row_count
    row_onehot = (rows_here[:, None] == jnp.arange(row_blocks, dtype=jnp.int32)[None, :]).astype(
        jnp.float32
    )
    col_onehot = (cols_here[:, None] == jnp.arange(col_blocks, dtype=jnp.int32)[None, :]).astype(
        jnp.float32
    )
    half_index = col_index % 2
    owner_flag = (col_index // 2 == row_index).astype(jnp.float32)

    def total_sum(values):
        return lax.psum(values, "row")

    def finish_factor(gram_matrix, block_rows):
        factor = jnp.linalg.cholesky(gram_matrix)
        solved = lax.linalg.triangular_solve(factor, block_rows, left_side=True, lower=True)
        return (solved, factor)

    basis, factor = finish_factor(
        total_sum(jnp.dot(start_block, start_block.T, precision=HIGH)), start_block
    )
    previous = jnp.zeros_like(basis)
    alpha_list = []
    beta_list = []
    for step_index in range(ITERS):
        rounded = basis.astype(jnp.bfloat16)
        own_columns = lax.dynamic_slice_in_dim(rounded, half_index * cell_cols, cell_cols, 1)
        col_vectors = from_root(own_columns, "row", col_index // 2)
        col_picked = jnp.take(
            col_vectors.reshape(vectors, col_blocks, tile_width), cols_here, axis=1
        )
        row_picked = jnp.take(rounded.reshape(vectors, row_blocks, tile_width), rows_here, axis=1)
        upper_part = jnp.einsum(
            "kij,vkj->vki", tiles_here, col_picked, preferred_element_type=jnp.float32
        )
        lower_part = jnp.einsum(
            "kij,vki->vkj", tiles_here, row_picked, preferred_element_type=jnp.float32
        )
        row_terms = jnp.einsum("kb,vki->vbi", row_onehot, upper_part, precision=HIGH).reshape(
            vectors, cell_rows
        )
        col_terms = jnp.einsum("kb,vkj->vbj", col_onehot, lower_part, precision=HIGH).reshape(
            vectors, cell_cols
        )
        mirrored = lax.psum(col_terms, "row")
        placed = lax.dynamic_update_slice_in_dim(
            jnp.zeros((vectors, cell_rows), jnp.float32),
            mirrored * owner_flag,
            half_index * cell_cols,
            1,
        )
        applied = lax.psum(row_terms + placed, "col")
        residual = applied - jnp.dot(factor.T, previous, precision=HIGH)
        alpha_block = total_sum(jnp.dot(basis, residual.T, precision=HIGH))
        residual = residual - jnp.dot(alpha_block.T, basis, precision=HIGH)
        gram_matrix = total_sum(jnp.dot(residual, residual.T, precision=HIGH))
        next_basis, factor = finish_factor(gram_matrix, residual)
        alpha_list.append(alpha_block)
        beta_list.append(factor.T)
        previous = basis
        basis = next_basis
    final_basis = basis * math.sqrt(total_rows)
    return (jnp.stack(alpha_list), jnp.stack(beta_list), final_basis)


def solution(mesh):
    in_specs = (
        P(None, "row"),
        P("row", "col", None, None, None),
        P("row", "col", None),
        P("row", "col", None),
    )
    out_specs = (P(), P(), P(None, "row"))
    return jax.shard_map(shards, mesh=mesh, in_specs=in_specs, out_specs=out_specs, check_vma=False)
```

profile of v0, /device:TPU:1, one launch (start us, length us, event | category | flops | bytes accessed | tf_op | source)
XLA Modules:
  0.0 1274.3 jit_solution(4181769950681915245)
XLA Ops:
  10.5 36.5 %psum.112 = f32[64,64]{0,1:T(8,128)S(1)} all-reduce(f32[64,64]{0,1:T(8,128)S(1)} %fusion.109), channel_id=1, replica_groups=mesh['row'=8,'col'=16] {'row'}, use_global_device_ids=true, to_apply=%region_0.1 | all-reduce | flops 4096 | bytes 32768 | tf_op jit(solution)/shard_map/psum | solution.py:43
  47.1 5.8 cholesky.74
  54.3 4.9 custom-call.8
  66.9 10.1 fusion.8
  77.0 7.5 fusion.20
  86.4 61.1 %all-reduce.10.cloned.1.call-done = bf16[64,16,256]{2,0,1:T(8,128)(2,1)} async-done(((bf16[64,16,256]{2,0,1:T(8,128)(2,1)}), bf16[64,16,256]{2,0,1:T(8,128)(2,1)}) %all-reduce.10.cloned.1.call-update) | async-done | bytes 524304 | tf_op jit(solution)/shard_map/psum | solution.py:16
  147.5 3.8 gather_fusion
  151.4 12.9 %fusion.10 = f32[128,64,256]{2,1,0:T(8,128)} fusion(bf16[1,1,128,256,256]{4,3,2,1,0:T(8,128)(2,1)} %param.12, bf16[128,64,256]{2,1,0:T(8,128)(2,1)} %gather_fusion, pred[128]{0:T(512)(128)(4,1)S(1)} %compare_and_fusion.1), kind=kOutput, calls=%fused_computation.16 | convolution fusion | flops 1075838976 | bytes 29360256 | tf_op jit(solution)/shard_map/kij,vkj->vki/dot_general | solution.py:64
  164.2 10.8 fusion.22
  176.2 60.2 %all-reduce.12.cloned.1.call-done = f32[64,4096]{1,0:T(8,128)} async-done(((f32[64,4096]{1,0:T(8,128)}), f32[64,4096]{1,0:T(8,128)}) %all-reduce.12.cloned.1.call-update) | async-done | bytes 1048592 | tf_op jit(solution)/shard_map/psum | solution.py:76
  239.2 126.1 %all-reduce.14.cloned.1.call-done = f32[64,8192]{1,0:T(8,128)} async-done(((f32[64,8192]{1,0:T(8,128)}), f32[64,8192]{1,0:T(8,128)}) %all-reduce.14.cloned.1.call-update) | async-done | bytes 2097168 | tf_op jit(solution)/shard_map/psum | solution.py:83
  365.3 3.3 convolution_subtract_fusion.5
  371.8 34.8 %psum.116 = f32[64,64]{1,0:T(8,128)S(1)} all-reduce(f32[64,64]{1,0:T(8,128)S(1)} %fusion.110), channel_id=1, replica_groups=mesh['row'=8,'col'=16] {'row'}, use_global_device_ids=true, to_apply=%region_6.11 | all-reduce | flops 4096 | bytes 32768 | tf_op jit(solution)/shard_map/psum | solution.py:43
  406.6 3.5 convolution_subtract_fusion.4
  413.3 29.7 %psum.117 = f32[64,64]{0,1:T(8,128)S(1)} all-reduce(f32[64,64]{0,1:T(8,128)S(1)} %fusion.111), channel_id=1, replica_groups=mesh['row'=8,'col'=16] {'row'}, use_global_device_ids=true, to_apply=%region_7.12 | all-reduce | flops 4096 | bytes 32768 | tf_op jit(solution)/shard_map/psum | solution.py:43
  443.1 5.8 cholesky.85
  450.3 4.9 custom-call.9
  455.2 4.9 fusion.107
  465.7 10.1 fusion.4
  475.8 7.5 fusion.16
  485.2 64.8 %all-reduce.16.cloned.1.call-done = bf16[64,16,256]{2,0,1:T(8,128)(2,1)} async-done(((bf16[64,16,256]{2,0,1:T(8,128)(2,1)}), bf16[64,16,256]{2,0,1:T(8,128)(2,1)}) %all-reduce.16.cloned.1.call-update) | async-done | bytes 524304 | tf_op jit(solution)/shard_map/psum | solution.py:16
  550.0 3.8 gather_fusion.2
  553.8 12.9 %fusion.6 = f32[128,64,256]{2,1,0:T(8,128)} fusion(bf16[1,1,128,256,256]{4,3,2,1,0:T(8,128)(2,1)} %param.12, bf16[128,64,256]{2,1,0:T(8,128)(2,1)} %gather_fusion.2, pred[128]{0:T(512)(128)(4,1)S(1)} %compare_and_fusion.1), kind=kOutput, calls=%fused_computation.12 | convolution fusion | flops 1075838976 | bytes 29360256 | tf_op jit(solution)/shard_map/kij,vkj->vki/dot_general | solution.py:64
  566.7 10.8 fusion.18
  580.0 58.5 %all-reduce.18.cloned.1.call-done = f32[64,4096]{1,0:T(8,128)} async-done(((f32[64,4096]{1,0:T(8,128)}), f32[64,4096]{1,0:T(8,128)}) %all-reduce.18.cloned.1.call-update) | async-done | bytes 1048592 | tf_op jit(solution)/shard_map/psum | solution.py:76
  641.2 126.3 %all-reduce.20.cloned.1.call-done = f32[64,8192]{1,0:T(8,128)} async-done(((f32[64,8192]{1,0:T(8,128)}), f32[64,8192]{1,0:T(8,128)}) %all-reduce.20.cloned.1.call-update) | async-done | bytes 2097168 | tf_op jit(solution)/shard_map/psum | solution.py:83
  767.4 4.3 convolution_subtract_fusion.3
  774.9 34.8 %psum.121 = f32[64,64]{1,0:T(8,128)S(1)} all-reduce(f32[64,64]{1,0:T(8,128)S(1)} %fusion.112), channel_id=1, replica_groups=mesh['row'=8,'col'=16] {'row'}, use_global_device_ids=true, to_apply=%region_11.16 | all-reduce | flops 4096 | bytes 32768 | tf_op jit(solution)/shard_map/psum | solution.py:43
  809.7 3.5 convolution_subtract_fusion.2
  816.4 29.7 %psum.122 = f32[64,64]{0,1:T(8,128)S(1)} all-reduce(f32[64,64]{0,1:T(8,128)S(1)} %fusion.113), channel_id=1, replica_groups=mesh['row'=8,'col'=16] {'row'}, use_global_device_ids=true, to_apply=%region_12.17 | all-reduce | flops 4096 | bytes 32768 | tf_op jit(solution)/shard_map/psum | solution.py:43
  846.2 5.8 cholesky.96
  853.4 4.9 custom-call.10
  858.3 4.9 fusion.108
  868.8 10.1 fusion
  878.9 7.5 fusion.12
  888.3 64.7 %all-reduce.22.cloned.1.call-done = bf16[64,16,256]{2,0,1:T(8,128)(2,1)} async-done(((bf16[64,16,256]{2,0,1:T(8,128)(2,1)}), bf16[64,16,256]{2,0,1:T(8,128)(2,1)}) %all-reduce.22.cloned.1.call-update) | async-done | bytes 524304 | tf_op jit(solution)/shard_map/psum | solution.py:16
  953.1 3.8 gather_fusion.4
  956.9 12.9 %fusion.2 = f32[128,64,256]{2,1,0:T(8,128)} fusion(bf16[1,1,128,256,256]{4,3,2,1,0:T(8,128)(2,1)} %param.12, bf16[128,64,256]{2,1,0:T(8,128)(2,1)} %gather_fusion.4, pred[128]{0:T(512)(128)(4,1)S(1)} %compare_and_fusion.1), kind=kOutput, calls=%fused_computation.8 | convolution fusion | flops 1075838976 | bytes 29360256 | tf_op jit(solution)/shard_map/kij,vkj->vki/dot_general | solution.py:64
  969.8 10.8 fusion.14
  983.1 58.9 %all-reduce.24.cloned.1.call-done = f32[64,4096]{1,0:T(8,128)} async-done(((f32[64,4096]{1,0:T(8,128)}), f32[64,4096]{1,0:T(8,128)}) %all-reduce.24.cloned.1.call-update) | async-done | bytes 1048592 | tf_op jit(solution)/shard_map/psum | solution.py:76
  1044.6 126.6 %all-reduce.26.cloned.1.call-done = f32[64,8192]{1,0:T(8,128)} async-done(((f32[64,8192]{1,0:T(8,128)}), f32[64,8192]{1,0:T(8,128)}) %all-reduce.26.cloned.1.call-update) | async-done | bytes 2097168 | tf_op jit(solution)/shard_map/psum | solution.py:83
  1171.2 4.3 convolution_subtract_fusion.1
  1178.7 34.8 %psum.126 = f32[64,64]{1,0:T(8,128)S(1)} all-reduce(f32[64,64]{1,0:T(8,128)S(1)} %fusion.114), channel_id=1, replica_groups=mesh['row'=8,'col'=16] {'row'}, use_global_device_ids=true, to_apply=%region_16.21 | all-reduce | flops 4096 | bytes 32768 | tf_op jit(solution)/shard_map/psum | solution.py:43
  1213.5 4.1 convolution_subtract_fusion
  1219.4 29.7 %psum.127 = f32[64,64]{0,1:T(8,128)S(1)} all-reduce(f32[64,64]{0,1:T(8,128)S(1)} %fusion.115), channel_id=1, replica_groups=mesh['row'=8,'col'=16] {'row'}, use_global_device_ids=true, to_apply=%region_17.22 | all-reduce | flops 4096 | bytes 32768 | tf_op jit(solution)/shard_map/psum | solution.py:43
  1249.2 5.8 cholesky.107
  1257.2 4.9 custom-call.11
  1262.1 4.8 convolution_multiply_fusion
  (110 shorter events, 66.5 us)
Async XLA Ops:
  7.2 1.6 copy-start
  7.2 140.3 %all-reduce.10.cloned.1.call-start = ((), (), s32[]{:S(2)}) async-start(), calls=%async_computation | async-start | bytes 1048576 | tf_op jit(solution)/shard_map/psum | solution.py:16
  62.5 1.5 copy-start.16
  63.4 172.9 %all-reduce.12.cloned.1.call-start = ((), (), s32[]{:S(2)}) async-start(), calls=%async_computation.1 | async-start | bytes 2097152 | tf_op jit(solution)/shard_map/psum | solution.py:76
  66.9 10.1 copy-start.15
  86.2 279.1 %all-reduce.14.cloned.1.call-start = ((), (), s32[]{:S(2)}) async-start(), calls=%async_computation.2 | async-start | bytes 4194304 | tf_op jit(solution)/shard_map/psum | solution.py:83
  237.8 1.3 copy-start.12
  239.1 130.9 %copy-start.2 = (f32[64,8192]{1,0:T(8,128)S(1)}, f32[64,8192]{1,0:T(8,128)}, u32[]{:S(2)}) copy-start(f32[64,8192]{1,0:T(8,128)} %get-tuple-element.20) | copy-start | bytes 6291460
  239.1 310.9 %all-reduce.16.cloned.1.call-start = ((), (), s32[]{:S(2)}) async-start(), calls=%async_computation.3 | async-start | bytes 1048576 | tf_op jit(solution)/shard_map/psum | solution.py:16
  368.6 1.4 copy-start.11
  410.1 1.3 copy-start.6
  460.0 1.6 copy-start.14
  461.1 177.4 %all-reduce.18.cloned.1.call-start = ((), (), s32[]{:S(2)}) async-start(), calls=%async_computation.4 | async-start | bytes 2097152 | tf_op jit(solution)/shard_map/psum | solution.py:76
  485.0 282.4 %all-reduce.20.cloned.1.call-start = ((), (), s32[]{:S(2)}) async-start(), calls=%async_computation.5 | async-start | bytes 4194304 | tf_op jit(solution)/shard_map/psum | solution.py:83
  641.1 311.9 %all-reduce.22.cloned.1.call-start = ((), (), s32[]{:S(2)}) async-start(), calls=%async_computation.6 | async-start | bytes 1048576 | tf_op jit(solution)/shard_map/psum | solution.py:16
  767.4 5.7 copy-start.3
  771.8 1.3 copy-start.9
  773.1 36.6 %copy-start.4 = (f32[64,8192]{1,0:T(8,128)S(1)}, f32[64,8192]{1,0:T(8,128)}, u32[]{:S(2)}) copy-start(f32[64,8192]{1,0:T(8,128)} %get-tuple-element.22) | copy-start | bytes 6291460
  813.3 1.3 copy-start.7
  863.1 1.6 copy-start.13
  864.3 177.7 %all-reduce.24.cloned.1.call-start = ((), (), s32[]{:S(2)}) async-start(), calls=%async_computation.7 | async-start | bytes 2097152 | tf_op jit(solution)/shard_map/psum | solution.py:76
  888.1 283.1 %all-reduce.26.cloned.1.call-start = ((), (), s32[]{:S(2)}) async-start(), calls=%async_computation.8 | async-start | bytes 4194304 | tf_op jit(solution)/shard_map/psum | solution.py:83
  1171.2 5.7 copy-start.10
  1175.6 1.3 copy-start.8
  1217.6 1.8 copy-start.5
  1257.2 10.4 copy-start.1
Sparse Core Ops, SparseCore 0:
  63.6 83.9 all-reduce.9
  150.2 86.1 all-reduce.11
  239.2 126.0 all-reduce.13
  461.3 88.6 all-reduce.15
  552.3 86.1 all-reduce.17
  641.4 125.9 all-reduce.19
  864.4 88.6 all-reduce.21
  955.7 86.1 all-reduce.23
  1045.2 125.9 all-reduce.25
where the time goes:
time: 1290 us; the launch traced here: 1270 us
  waiting for transfers between devices  747 us (58%)
  blocking collectives  230 us (18%)
  matrix products  177 us (14%)
  other arithmetic  55.9 us (4%)
  local copies, waits for them, and re-layouts  46.9 us (4%)
  between operations  14.6 us (1%)
    psum x3, waiting for transfers between devices, shards(): applied = lax.psum(row_terms + placed, 'col')  379 us
    psum x7, blocking collectives, total_sum(): return lax.psum(values, 'row')  230 us
    psum x3, waiting for transfers between devices, from_root(): return lax.psum(kept, axis)  191 us
    psum x3, waiting for transfers between devices, shards(): mirrored = lax.psum(col_terms, 'row')  178 us
    dot_general x3, matrix products, shards(): jnp.einsum('kij,vkj->vki', tiles_here, col_picked, preferred_element_type...  38.6 us
    dot_general x3, matrix products, shards(): jnp.einsum('kb,vki->vbi', row_onehot, upper_part, precision=HIGH)  32.3 us
    dot_general x3, matrix products, shards(): jnp.einsum('kij,vki->vkj', tiles_here, row_picked, preferred_element_type...  30.4 us
    another operation x12, other arithmetic, finish_factor(): factor = jnp.linalg.cholesky(gram_matrix)  26.1 us
  transfers between devices with their start and end apart: 9, of which 9 were waited for; matrix products, arithmetic and copies ran while one was open for 12% of the time, Pallas kernels for 0%

commit v1 on v0

v1 whole, which is shorter than its diff:
```python
import math

import jax
import jax.numpy as jnp
from jax import lax
from jax.experimental import pallas as pl
from jax.experimental.pallas import tpu as pltpu
from jax.sharding import PartitionSpec as P

ITERS = 3
HIGH = lax.Precision.HIGHEST
MESH = pl.DeviceIdType.MESH
F32 = jnp.float32
BF16 = jnp.bfloat16
NT = (((1,), (1,)), ((), ()))
NN = (((1,), (0,)), ((), ()))
UNROLL = 16


def dot_high(a, b, dims=NN):
    return lax.dot_general(a, b, dims, precision=HIGH, preferred_element_type=F32)


def factor_rows(rows):
    lane = lax.broadcasted_iota(jnp.int32, (8, 128), 1)
    sub = lax.broadcasted_iota(jnp.int32, (8, 128), 0)
    for j in range(64):
        at, inner = divmod(j, 8)
        pivot_row = rows[at][inner : inner + 1, :]
        inverse = 1.0 / pivot_row[:, j : j + 1]
        for i in range(at, 8):
            scale = jnp.broadcast_to(rows[i][:, j : j + 1] * inverse, (8, 128))
            if i == at:
                scale = jnp.where(sub > inner, scale, 0.0)
            rows[i] = rows[i] - scale * pivot_row
    done = []
    for i in range(8):
        diagonal = jnp.sum(jnp.where(lane == sub + 8 * i, rows[i], 0.0), axis=1, keepdims=True)
        scaled = rows[i] * lax.rsqrt(diagonal)
        done.append(jnp.where((lane < sub + 8 * i) & (lane < 64), 0.0, scaled))
    return done


def kernel(
    perm_r, col_of, keep_r, last_r, has_r, perm_c, row_of, keep_c, last_c, has_c,
    start, tiles_hbm,
    alphas, betas, final,
    tiles, slots, v_row, v_col, upper, lower, low_send,
    half_in, x_send, x_in, y_in, row_in, col_in, col_sum,
    wq, prev, fact, g_send, g_one, g_two, g_three,
    load_sem, start_sem,
    ag1_s, ag1_r, agx_s, agx_r, agy_s, agy_r, agc_s, agc_r,
    rsc_s, rsc_r, rsx_s, rsx_r, rsy_s, rsy_r, rsf_s, rsf_r,
    g1_s, g1_r, g2_s, g2_r, g3_s, g3_r,
):
    r = lax.axis_index("row")
    c = lax.axis_index("col")
    zh, y = r // 4, r % 4
    x, zl, k = c // 4, (c // 2) % 2, c % 2
    core = (r, c + 1 - 2 * k)
    pair = (r, c + 2 - 4 * zl)
    x_at = [(x + i) % 4 for i in range(4)]
    y_at = [(y + i) % 4 for i in range(4)]
    x_dev = [(r, i * 4 + zl * 2 + k) for i in x_at]
    y_dev = [(zh * 4 + i, c) for i in y_at]
    holders = [(e * 4 + x, (zh * 2 + y // 2) * 4 + (y % 2) * 2 + (1 - k)) for e in (0, 1)]
    owners = [(2 * x + zl, y * 4 + e * 2 + (1 - k)) for e in (0, 1)]
    mine = (1 - k) * 16
    other = k * 16
    home = mine + 4 * x + 2 * zl

    load = pltpu.make_async_copy(tiles_hbm, tiles, load_sem)
    load.start()
    first = pltpu.make_async_copy(
        start.at[:, pl.ds(pl.multiple_of(home * 256, 512), 512)], wq.at[pl.ds(0, 64), :], start_sem
    )
    first.start()

    barrier = pltpu.get_barrier_semaphore()

    def greet_row(i, _):
        pl.semaphore_signal(barrier, inc=1, device_id=(r, (c + i) % 16), device_id_type=MESH)
        return 0

    def greet_col(i, _):
        pl.semaphore_signal(barrier, inc=1, device_id=((r + i) % 8, c), device_id_type=MESH)
        return 0

    lax.fori_loop(1, 16, greet_row, 0)
    lax.fori_loop(1, 8, greet_col, 0)
    for device in holders + owners:
        pl.semaphore_signal(barrier, inc=1, device_id=device, device_id_type=MESH)
    wq[pl.ds(64, 64), :] = jnp.zeros((64, 512), F32)
    prev[...] = jnp.zeros_like(prev)
    first.wait()
    pl.semaphore_wait(barrier, 26)

    def remote(src, dst, s, d, device):
        return pltpu.make_async_remote_copy(
            src_ref=src, dst_ref=dst, send_sem=s, recv_sem=d, device_id=device, device_id_type=MESH
        )

    def sum_over_devices():
        gram = dot_high(wq[pl.ds(0, 64), :], wq[...], NT)
        for i in range(16):
            g_send[i] = gram[4 * i : 4 * i + 4, :]
        g_one[c] = g_send[c]

        def one(i):
            p = (c + i) % 16
            return remote(g_send.at[p], g_one.at[c], g1_s.at[i], g1_r.at[c], (r, p))

        def one_in(i):
            p = (c + i) % 16
            return remote(g_send.at[p], g_one.at[p], g1_s.at[i], g1_r.at[p], (r, p))

        def two(i):
            p = (r + i) % 8
            return remote(g_two.at[r], g_two.at[r], g2_s.at[i], g2_r.at[r], (p, c))

        def two_in(i):
            p = (r + i) % 8
            return remote(g_two.at[p], g_two.at[p], g2_s.at[i], g2_r.at[p], (p, c))

        def three(i):
            p = (c + i) % 16
            return remote(g_three.at[c], g_three.at[c], g3_s.at[i], g3_r.at[c], (r, p))

        def three_in(i):
            p = (c + i) % 16
            return remote(g_three.at[p], g_three.at[p], g3_s.at[i], g3_r.at[p], (r, p))

        def each(count, do):
            def step(i, _):
                do(i)
                return 0

            lax.fori_loop(1, count, step, 0)

        each(16, lambda i: one(i).start())
        each(16, lambda i: one_in(i).wait_recv())
        g_two[r] = jnp.sum(g_one[...], axis=0)
        each(8, lambda i: two(i).start())
        each(8, lambda i: two_in(i).wait_recv())
        g_three[c] = jnp.sum(g_two[...], axis=0)
        each(16, lambda i: three(i).start())
        each(16, lambda i: three_in(i).wait_recv())
        each(16, lambda i: one(i).wait_send())
        each(8, lambda i: two(i).wait_send())
        each(16, lambda i: three(i).wait_send())
        for i in range(16):
            fact[pl.ds(4 * i, 4), :] = g_three[i]

    def orthonormalize(keep):
        sum_over_devices()
        cross = fact[:, 64:128]
        keep(0, cross)
        fact[:, 0:64] = fact[:, 0:64] - dot_high(cross, cross, NT)
        eye_r = lax.broadcasted_iota(jnp.int32, (64, 64), 0)
        eye_c = lax.broadcasted_iota(jnp.int32, (64, 64), 1)
        fact[:, 64:128] = (eye_r == eye_c).astype(F32)
        done = factor_rows([fact[8 * i : 8 * i + 8, :] for i in range(8)])
        for i in range(8):
            fact[8 * i : 8 * i + 8, :] = done[i]
        keep(1, fact[:, 0:64])
        old = wq[pl.ds(64, 64), :]
        residual = wq[pl.ds(0, 64), :] - dot_high(cross, old)
        new = dot_high(fact[:, 64:128], residual)
        prev[...] = old
        wq[pl.ds(64, 64), :] = new
        rounded = new.astype(BF16)
        v_row[home] = rounded[:, 0:256]
        v_row[home + 1] = rounded[:, 256:512]

    def gather_x_begin():
        block = v_row.at[pl.ds(home, 2)]
        sent = [remote(block, block, ag1_s.at[0], ag1_r.at[0], pair)]
        for i in (1, 2, 3):
            sent.append(remote(block, block, agx_s.at[i, 0], agx_r.at[x, zl], x_dev[i]))
        return sent

    def gather_x_forward():
        theirs = mine + 4 * x + 2 * (1 - zl)
        block = v_row.at[pl.ds(theirs, 2)]
        remote(block, block, ag1_s.at[0], ag1_r.at[0], pair).wait_recv()
        sent = []
        for i in (1, 2, 3):
            sent.append(remote(block, block, agx_s.at[i, 1], agx_r.at[x, 1 - zl], x_dev[i]))
        whole = v_row.at[pl.ds(mine + 4 * x, 4)]
        sent.append(remote(whole, whole, agc_s.at[0], agc_r.at[x], core))
        return sent

    def gather_x_finish():
        sent = []
        for i in (1, 3, 2):
            for e in (0, 1):
                block = v_row.at[pl.ds(mine + 4 * x_at[i] + 2 * e, 2)]
                remote(block, block, agx_s.at[i, 0], agx_r.at[x_at[i], e], x_dev[i]).wait_recv()
            whole = v_row.at[pl.ds(mine + 4 * x_at[i], 4)]
            copy = remote(whole, whole, agc_s.at[i], agc_r.at[x_at[i]], core)
            copy.start()
            sent.append(copy)
        return sent

    def gather_core_wait():
        for i in range(4):
            whole = v_row.at[pl.ds(other + 4 * x_at[i], 4)]
            remote(whole, whole, agc_s.at[i], agc_r.at[x_at[i]], core).wait_recv()

    def multiply_up(low, high, running):
        def step(j, acc):
            for i in range(UNROLL):
                p = j * UNROLL + i
                part = lax.dot_general(
                    v_col[col_of[p]], tiles[perm_r[p]], NT, preferred_element_type=F32
                )
                acc = acc * keep_r[p] + part
                slots[p] = acc
            return acc

        return lax.fori_loop(low, high, step, running)

    def multiply_down(low, high, running):
        def step(j, acc):
            for i in range(UNROLL):
                p = j * UNROLL + i
                part = lax.dot_general(
                    v_row[row_of[p]], tiles[perm_c[p]], NN, preferred_element_type=F32
                )
                acc = acc * keep_c[p] + part
                slots[p] = acc
            return acc

        return lax.fori_loop(low, high, step, running)

    def iterate(step_at, keep):
        orthonormalize(keep)
        sent = gather_x_begin()
        block = v_row.at[pl.ds(home, 2)]
        for e in (0, 1):
            there = v_col.at[pl.ds(4 * x + 2 * zl, 2)]
            sent.append(remote(block, there, ag1_s.at[1 + e], ag1_r.at[1 + zl], holders[e]))
        for copy in sent[::-1]:
            copy.start()
        for e in (0, 1):
            part = v_col.at[pl.ds(4 * y + 2 * e, 2)]
            remote(part, part, ag1_s.at[1], ag1_r.at[1 + e], owners[e]).wait_recv()
            for i in (2, 1, 3):
                copy = remote(part, part, agy_s.at[i, e], agy_r.at[y, e], y_dev[i])
                copy.start()
                sent.append(copy)
        forward = gather_x_forward()
        for copy in forward:
            copy.start()
        sent += forward

        @pl.when(step_at == 0)
        def _():
            load.wait()

        for i in (1, 3, 2):
            for e in (0, 1):
                part = v_col.at[pl.ds(4 * y_at[i] + 2 * e, 2)]
                remote(part, part, agy_s.at[i, e], agy_r.at[y_at[i], e], y_dev[i]).wait_recv()

        half = 64 // UNROLL
        zero = jnp.zeros((64, 256), F32)
        running = multiply_up(0, half, zero)
        sent += gather_x_finish()
        multiply_up(half, 2 * half, running)

        def pick_up(b, _):
            upper[b] = slots[last_r[b]] * has_r[b]
            return 0

        lax.fori_loop(0, 32, pick_up, 0)
        for i in (1, 2, 3, 0):
            copy = remote(
                upper.at[pl.ds(other + 4 * x_at[i], 4)], half_in.at[pl.ds(4 * x_at[i], 4)],
                rsc_s.at[i], rsc_r.at[x_at[i]], core,
            )
            copy.start()
            sent.append(copy)
        gather_core_wait()
        running = multiply_down(0, half, zero)
        for i in (2, 1, 3, 0):
            q = x_at[i]
            theirs = half_in.at[pl.ds(4 * q, 4)]
            remote(theirs, theirs, rsc_s.at[i], rsc_r.at[q], core).wait_recv()

            def add_half(b, _):
                total = upper[mine + 4 * q + b] + half_in[4 * q + b]
                if i:
                    x_send[4 * i + b] = total.astype(BF16)
                else:
                    upper[mine + 4 * q + b] = total
                return 0

            lax.fori_loop(0, 4, add_half, 0)
            if i:
                copy = remote(
                    x_send.at[pl.ds(4 * i, 4)], x_in.at[pl.ds(4 * (4 - i), 4)],
                    rsx_s.at[i], rsx_r.at[4 - i], x_dev[i],
                )
                copy.start()
                sent.append(copy)
        multiply_down(half, 2 * half, running)

        def pick_down(b, _):
            total = slots[last_c[b]] * has_c[b]
            lower[b] = total
            low_send[b] = total.astype(BF16)
            return 0

        lax.fori_loop(0, 16, pick_down, 0)
        for i in (2, 1, 3):
            copy = remote(
                low_send.at[pl.ds(4 * y_at[i], 4)], y_in.at[pl.ds(4 * (4 - i), 4)],
                rsy_s.at[i], rsy_r.at[4 - i], y_dev[i],
            )
            copy.start()
            sent.append(copy)
        for i in (1, 3, 2):
            part = x_in.at[pl.ds(4 * i, 4)]
            remote(part, part, rsx_s.at[i], rsx_r.at[i], x_dev[i]).wait_recv()

        def add_x(b, _):
            at = mine + 4 * x + b
            upper[at] = (
                upper[at]
                + x_in[4 + b].astype(F32)
                + x_in[8 + b].astype(F32)
                + x_in[12 + b].astype(F32)
            )
            return 0

        lax.fori_loop(0, 4, add_x, 0)
        copy = remote(
            upper.at[pl.ds(mine + 4 * x + 2 * (1 - zl), 2)], row_in, rsf_s.at[0], rsf_r.at[0], pair
        )
        copy.start()
        sent.append(copy)
        for i in (1, 3, 2):
            part = y_in.at[pl.ds(4 * i, 4)]
            remote(part, part, rsy_s.at[i], rsy_r.at[i], y_dev[i]).wait_recv()

        def add_y(b, _):
            col_sum[b] = (
                lower[4 * y + b]
                + y_in[4 + b].astype(F32)
                + y_in[8 + b].astype(F32)
                + y_in[12 + b].astype(F32)
            )
            return 0

        lax.fori_loop(0, 4, add_y, 0)
        for e in (0, 1):
            copy = remote(
                col_sum.at[pl.ds(2 * e, 2)], col_in.at[zh], rsf_s.at[1 + e], rsf_r.at[1 + zh], owners[e]
            )
            copy.start()
            sent.append(copy)
        carried = dot_high(fact[:, 0:64], prev[...])
        remote(row_in, row_in, rsf_s.at[0], rsf_r.at[0], pair).wait_recv()
        for e in (0, 1):
            part = col_in.at[e]
            remote(part, part, rsf_s.at[1 + e], rsf_r.at[1 + e], holders[e]).wait_recv()
        for b in (0, 1):
            applied = upper[home + b] + row_in[b] + col_in[0, b] + col_in[1, b]
            wq[pl.ds(0, 64), 256 * b : 256 * b + 256] = applied - carried[:, 256 * b : 256 * b + 256]
        for copy in sent:
            copy.wait_send()

    def keep_in_loop(step_at):
        def keep(which, value):
            @pl.when(step_at > 0)
            def _():
                if which == 0:
                    alphas[step_at - 1] = value.T
                else:
                    betas[step_at - 1] = value

        return keep

    def body(step_at, _):
        iterate(step_at, keep_in_loop(step_at))
        return 0

    lax.fori_loop(0, ITERS, body, 0)

    def keep_last(which, value):
        if which == 0:
            alphas[ITERS - 1] = value.T
        else:
            betas[ITERS - 1] = value

    orthonormalize(keep_last)
    sent = gather_x_begin()
    for copy in sent:
        copy.start()
    forward = gather_x_forward()
    for copy in forward:
        copy.start()
    sent += forward + gather_x_finish()
    gather_core_wait()
    final[...] = v_row[...]
    for copy in sent:
        copy.wait_send()


def order_by(keys, others, blocks):
    count = keys.shape[0]
    at = jnp.arange(count, dtype=jnp.int32)
    unique = keys * count + at
    rank = jnp.sum((unique[None, :] < unique[:, None]).astype(jnp.int32), axis=1)
    here = (rank[None, :] == at[:, None]).astype(jnp.int32)
    perm = jnp.sum(here * at[None, :], axis=1)
    other = jnp.sum(here * others[None, :], axis=1)
    dest = jnp.sum(here * keys[None, :], axis=1)
    before = jnp.concatenate([jnp.full((1,), -1, jnp.int32), dest[:-1]])
    keep = (dest == before).astype(F32)
    block = jnp.arange(blocks, dtype=jnp.int32)
    upto = jnp.sum((keys[None, :] <= block[:, None]).astype(jnp.int32), axis=1)
    has = jnp.any(keys[None, :] == block[:, None], axis=1).astype(F32)
    return perm, other, keep, jnp.maximum(upto - 1, 0), has


def shards(start_block, tile_values, tile_rows, tile_cols):
    tiles = tile_values[0, 0]
    rows, cols = tile_rows[0, 0], tile_cols[0, 0]
    by_row = order_by(rows, cols, 32)
    by_col = order_by(cols, rows, 16)
    smem = pl.BlockSpec(memory_space=pltpu.SMEM)
    vmem = pl.BlockSpec(memory_space=pltpu.VMEM)
    hbm = pl.BlockSpec(memory_space=pl.ANY)
    dma = pltpu.SemaphoreType.DMA
    alphas, betas, final = pl.pallas_call(
        kernel,
        out_shape=[
            jax.ShapeDtypeStruct((ITERS, 64, 64), F32),
            jax.ShapeDtypeStruct((ITERS, 64, 64), F32),
            jax.ShapeDtypeStruct((32, 64, 256), BF16),
        ],
        in_specs=[smem] * 10 + [hbm, hbm],
        out_specs=[vmem] * 3,
        scratch_shapes=[
            pltpu.VMEM((128, 256, 256), BF16),
            pltpu.VMEM((128, 64, 256), F32),
            pltpu.VMEM((32, 64, 256), BF16),
            pltpu.VMEM((16, 64, 256), BF16),
            pltpu.VMEM((32, 64, 256), F32),
            pltpu.VMEM((16, 64, 256), F32),
            pltpu.VMEM((16, 64, 256), BF16),
            pltpu.VMEM((16, 64, 256), F32),
            pltpu.VMEM((16, 64, 256), BF16),
            pltpu.VMEM((16, 64, 256), BF16),
            pltpu.VMEM((16, 64, 256), BF16),
            pltpu.VMEM((2, 64, 256), F32),
            pltpu.VMEM((2, 2, 64, 256), F32),
            pltpu.VMEM((4, 64, 256), F32),
            pltpu.VMEM((128, 512), F32),
            pltpu.VMEM((64, 512), F32),
            pltpu.VMEM((64, 128), F32),
            pltpu.VMEM((16, 4, 128), F32),
            pltpu.VMEM((16, 4, 128), F32),
            pltpu.VMEM((8, 4, 128), F32),
            pltpu.VMEM((16, 4, 128), F32),
            dma, dma,
            dma((3,)), dma((3,)), dma((4, 2)), dma((4, 2)), dma((4, 2)), dma((4, 2)),
            dma((4,)), dma((4,)),
            dma((4,)), dma((4,)), dma((4,)), dma((4,)), dma((4,)), dma((4,)), dma((3,)), dma((3,)),
            dma((16,)), dma((16,)), dma((8,)), dma((8,)), dma((16,)), dma((16,)),
        ],
        compiler_params=pltpu.CompilerParams(
            collective_id=0, has_side_effects=True, vmem_limit_bytes=56 * 1024 * 1024
        ),
    )(*by_row, *by_col, start_block, tiles)
    total_rows = start_block.shape[1] * lax.axis_size("row")
    basis = final.transpose(1, 0, 2).reshape(start_block.shape).astype(F32)
    return alphas, betas, basis * math.sqrt(total_rows)


def solution(mesh):
    in_specs = (
        P(None, "row"),
        P("row", "col", None, None, None),
        P("row", "col", None),
        P("row", "col", None),
    )
    out_specs = (P(), P(), P(None, "row"))
    return jax.shard_map(shards, mesh=mesh, in_specs=in_specs, out_specs=out_specs, check_vma=False)
```

time: 1290 us -> 282 us (0.22); the launches traced: 1270 us -> 282 us
  waiting for transfers between devices: 747 us -> 0 us
  Pallas kernels: 0 us -> 268 us
  blocking collectives: 230 us -> 0 us
  matrix products: 177 us -> 0 us
  other arithmetic: 55.9 us -> 10.5 us
  local copies, waits for them, and re-layouts: 46.9 us -> 2.79 us
  between operations: 14.6 us -> 0.68 us
    psum x9 -> x0, waiting for transfers between devices: 747 us -> none  [the longest x3 379 us: shards(): applied = lax.psum(row_terms + placed, 'col')]
    pallas_call x0 -> x1, Pallas kernels: none -> 268 us  [shards(): pl.pallas_call(kernel, out_shape=[jax.ShapeDtypeStruct((ITERS, 64, 64), F...]
    psum x7 -> x0, blocking collectives: 230 us -> none  [total_sum(): return lax.psum(values, 'row')]
    dot_general x25 -> x0, matrix products: 160 us -> none  [the longest x3 38.6 us: shards(): jnp.einsum('kij,vkj->vki', tiles_here, col_picked, preferred_element_type...]
    another operation x22 -> x0, other arithmetic: 48.9 us -> none  [the longest x12 26.1 us: finish_factor(): factor = jnp.linalg.cholesky(gram_matrix)]
    unnamed x41 -> x6, local copies, waits for them, and re-layouts: 21.2 us -> 1.29 us
    gather x6 -> x0, local copies, waits for them, and re-layouts: 19.7 us -> none  [the longest x3 11.5 us: shards(): jnp.take(col_vectors.reshape(vectors, col_blocks, tile_width), cols_here,...]
    another operation x4 -> x0, matrix products: 17.8 us -> none  [finish_factor(): lax.linalg.triangular_solve(factor, block_rows, left_side=True, lower=True)]
  transfers between devices with their start and end apart: 9 -> 0, of which waited for: 9 -> 0; matrix products, arithmetic and copies ran while one was open for 12% -> 0% of each run, Pallas kernels for 0% -> 0%
where the time goes in v1:
time: 282 us
  Pallas kernels  268 us (95%)
  other arithmetic  10.5 us (4%)
    pallas_call x1, Pallas kernels, shards(): pl.pallas_call(kernel, out_shape=[jax.ShapeDtypeStruct((ITERS, 64, 64), F...  268 us

profile of v1, /device:TPU:1, one launch (start us, length us, event | category | flops | bytes accessed | tf_op | source)
XLA Modules:
  0.0 281.5 jit_solution(8767373479276941625)
XLA Ops:
  0.6 0.8 convert_reduce_fusion.2
  1.4 0.6 add_maximum_fusion.1.last_r
  2.0 0.8 fusion
  2.8 0.6 convert_element_type.34.has_r
  3.3 0.7 iota_add_fusion.1
  4.0 0.2 convert_reduce_fusion.1
  4.2 0.8 convert_reduce_fusion.3
  4.9 0.5 add_maximum_fusion.last_c
  5.5 0.8 fusion.1
  6.2 0.6 convert_element_type.38.has_c
  6.8 0.7 iota_add_fusion
  7.5 0.2 convert_reduce_fusion
  7.7 1.4 select_reduce_fusion
  9.0 0.7 compare_convert_fusion
  9.7 267.5 %shard_map.67 = (f32[3,64,64]{2,1,0:T(8,128)}, f32[3,64,64]{2,1,0:T(8,128)}, bf16[32,64,256]{2,1,0:T(8,128)(2,1)}) custom-call(s32[128]{0:T(128)} %get-tuple-element.13.perm_r, s32[128]{0:T(128)} %get-tuple-element.10.col_of, f32[128]{0:T(128)} %get-tuple-element.16.keep_r, s32[32]{0:T(128)} %add_maximum_fusion.1.last_r, f32[32]{0:T(128)} %convert_element_type.34.has_r, ...), custom_call_target="tpu_custom_call" | custom-call | tf_op jit(solution)/shard_map/pallas_call | solution.py:437
  277.2 1.4 multiply_bitcast_fusion
  278.7 0.0 copy-start.1
  278.7 0.0 copy-start
  278.7 1.5 copy.9
  280.2 0.0 copy-done.1
  280.2 0.6 copy.12
  280.9 0.0 copy-done
  280.9 0.6 copy.13
Async XLA Ops:
  278.7 1.5 copy-start.1
  278.7 2.2 copy-start

commit v2 on v1

v2 whole, which is shorter than its diff:
```python
import math

import jax
import jax.numpy as jnp
from jax import lax
from jax.experimental import pallas as pl
from jax.experimental.pallas import tpu as pltpu
from jax.sharding import PartitionSpec as P

ITERS = 3
HIGH = lax.Precision.HIGHEST
MESH = pl.DeviceIdType.MESH
F32 = jnp.float32
BF16 = jnp.bfloat16
NT = (((1,), (1,)), ((), ()))
NN = (((1,), (0,)), ((), ()))
UNROLL = 16


def dot_high(a, b, dims=NN):
    return lax.dot_general(a, b, dims, precision=HIGH, preferred_element_type=F32)


def factor_rows(rows):
    lane = lax.broadcasted_iota(jnp.int32, (8, 128), 1)
    sub = lax.broadcasted_iota(jnp.int32, (8, 128), 0)
    for j in range(64):
        at, inner = divmod(j, 8)
        pivot_row = rows[at][inner : inner + 1, :]
        inverse = 1.0 / pivot_row[:, j : j + 1]
        for i in range(at, 8):
            scale = jnp.broadcast_to(rows[i][:, j : j + 1] * inverse, (8, 128))
            if i == at:
                scale = jnp.where(sub > inner, scale, 0.0)
            rows[i] = rows[i] - scale * pivot_row
    done = []
    for i in range(8):
        diagonal = jnp.sum(jnp.where(lane == sub + 8 * i, rows[i], 0.0), axis=1, keepdims=True)
        scaled = rows[i] * lax.rsqrt(diagonal)
        done.append(jnp.where((lane < sub + 8 * i) & (lane < 64), 0.0, scaled))
    return done


def order_by(keys, others):
    lane = lax.broadcasted_iota(jnp.int32, (128, 128), 1)
    sub = lax.broadcasted_iota(jnp.int32, (128, 128), 0)
    key_l = jnp.broadcast_to(keys, (128, 128))
    key_s = key_l.T
    other_s = jnp.broadcast_to(others, (128, 128)).T
    smaller = (key_l * 128 + lane) < (key_s * 128 + sub)
    rank = jnp.sum(smaller.astype(jnp.int32), axis=1, keepdims=True)

    def pick(hit, values):
        return jnp.sum(jnp.where(hit, values, 0), axis=0, keepdims=True)

    here = rank == lane
    perm = pick(here, sub)
    other = pick(here, other_s)
    dest = pick(here, key_s)
    before = pick(rank == lane - 1, key_s)
    upto = pick(key_s <= lane, jnp.ones_like(lane))
    count = pick(key_s == lane, jnp.ones_like(lane))
    return (
        perm, other, jnp.maximum(upto - 1, 0),
        (dest == before).astype(F32), (count > 0).astype(F32),
    )


def kernel(
    tile_rows, tile_cols, start, tiles_hbm,
    alphas, betas, final,
    tiles, slots, v_r0, v_r1, v_r2, v_r3, v_c0, v_c1, v_c2, upper, lower, low_send,
    half_in, x_send, x_in, y_in, row_in, col_in, col_sum,
    wq, q_new, applied_old, offset, carried, fact, cross, q_row,
    g_send, g_one, g_two, g_two_alone, g_three,
    order_i, order_f, where_i, where_f,
    load_sem, start_sem, order_sem,
    ag1_s, ag1_r, agx_s, agx_r, agy_s, agy_r, agc_s, agc_r,
    rsc_s, rsc_r, rsx_s, rsx_r, rsy_s, rsy_r, rsf_s, rsf_r,
    g1_s, g1_r, g2_s, g2_r, g2l_s, g2l_r, g3_s, g3_r,
):
    r = lax.axis_index("row")
    c = lax.axis_index("col")
    zh, y = r // 4, r % 4
    x, zl, k = c // 4, (c // 2) % 2, c % 2
    core = (r, c + 1 - 2 * k)
    pair = (r, c + 2 - 4 * zl)
    x_at = [(x + i) % 4 for i in range(4)]
    y_at = [(y + i) % 4 for i in range(4)]
    x_dev = [(r, i * 4 + zl * 2 + k) for i in x_at]
    y_dev = [(zh * 4 + i, c) for i in y_at]
    holders = [(e * 4 + x, (zh * 2 + y // 2) * 4 + (y % 2) * 2 + (1 - k)) for e in (0, 1)]
    owners = [(2 * x + zl, y * 4 + e * 2 + (1 - k)) for e in (0, 1)]
    mine = (1 - k) * 16
    other = k * 16
    home = mine + 4 * x + 2 * zl
    top, bottom = pl.ds(0, 64), pl.ds(64, 64)
    v_row, v_col = (v_r0, v_r1, v_r2, v_r3), (v_c0, v_c1, v_c2)

    first = pltpu.make_async_copy(
        start.at[:, pl.ds(pl.multiple_of(home * 256, 512), 512)], wq.at[top, :], start_sem
    )
    first.start()
    load = pltpu.make_async_copy(tiles_hbm, tiles, load_sem)
    load.start()

    barrier = pltpu.get_barrier_semaphore()

    def greet_row(i, _):
        pl.semaphore_signal(barrier, inc=1, device_id=(r, (c + i) % 16), device_id_type=MESH)
        return 0

    def greet_col(i, _):
        pl.semaphore_signal(barrier, inc=1, device_id=((r + i) % 8, c), device_id_type=MESH)
        return 0

    lax.fori_loop(1, 16, greet_row, 0)
    lax.fori_loop(1, 8, greet_col, 0)
    for device in holders + owners:
        pl.semaphore_signal(barrier, inc=1, device_id=device, device_id_type=MESH)
    wq[bottom, :] = jnp.zeros((64, 512), F32)
    applied_old[...] = jnp.zeros_like(applied_old)
    first.wait()
    pl.semaphore_wait(barrier, 26)

    def remote(src, dst, s, d, device):
        return pltpu.make_async_remote_copy(
            src_ref=src, dst_ref=dst, send_sem=s, recv_sem=d, device_id=device, device_id_type=MESH
        )

    def each(count, do):
        def step(i, _):
            do(i)
            return 0

        lax.fori_loop(1, count, step, 0)

    def one(i):
        p = (c + i) % 16
        return remote(g_send.at[p], g_one.at[c], g1_s.at[i], g1_r.at[c], (r, p))

    def one_in(i):
        p = (c + i) % 16
        return remote(g_send.at[p], g_one.at[p], g1_s.at[i], g1_r.at[p], (r, p))

    def two(i, last):
        p = (r + i) % 8
        buffer, s, d = (g_two_alone, g2l_s, g2l_r) if last else (g_two, g2_s, g2_r)
        return remote(buffer.at[r], buffer.at[r], s.at[i], d.at[r], (p, c))

    def two_in(i, last):
        p = (r + i) % 8
        buffer, s, d = (g_two_alone, g2l_s, g2l_r) if last else (g_two, g2_s, g2_r)
        return remote(buffer.at[p], buffer.at[p], s.at[i], d.at[p], (p, c))

    def three(i):
        p = (c + i) % 16
        return remote(g_three.at[c], g_three.at[c], g3_s.at[i], g3_r.at[c], (r, p))

    def three_in(i):
        p = (c + i) % 16
        return remote(g_three.at[p], g_three.at[p], g3_s.at[i], g3_r.at[p], (r, p))

    def gram_begin():
        gram = dot_high(wq[top, :], wq[...], NT)
        for i in range(16):
            g_send[i] = gram[4 * i : 4 * i + 4, :]
        each(16, lambda i: one(i).start())
        g_one[c] = g_send[c]

    def gram_second(last=False):
        each(16, lambda i: one_in(i).wait_recv())
        (g_two_alone if last else g_two)[r] = jnp.sum(g_one[...], axis=0)
        each(8, lambda i: two(i, last).start())

    def gram_third(last=False):
        each(8, lambda i: two_in(i, last).wait_recv())
        g_three[c] = jnp.sum((g_two_alone if last else g_two)[...], axis=0)
        each(16, lambda i: three(i).start())

    def gram_end(at, last=False):
        each(16, lambda i: three_in(i).wait_recv())
        for i in range(16):
            fact[at, pl.ds(4 * i, 4), :] = g_three[i]
        turned = fact[at, :, 64:128]
        cross[at] = turned
        fact[at, :, 0:64] = fact[at, :, 0:64] - dot_high(turned, turned, NT)
        eye_r = lax.broadcasted_iota(jnp.int32, (64, 64), 0)
        eye_c = lax.broadcasted_iota(jnp.int32, (64, 64), 1)
        fact[at, :, 64:128] = (eye_r == eye_c).astype(F32)
        done = factor_rows([fact[at, 8 * i : 8 * i + 8, :] for i in range(8)])
        for i in range(8):
            fact[at, 8 * i : 8 * i + 8, :] = done[i]
        each(16, lambda i: one(i).wait_send())
        each(8, lambda i: two(i, last).wait_send())
        each(16, lambda i: three(i).wait_send())

    def place(at):
        rounded = wq[top, :].astype(BF16)
        v_row[at][home] = rounded[:, 0:256]
        v_row[at][home + 1] = rounded[:, 256:512]

    def gather_x_begin(at):
        block = v_row[at].at[pl.ds(home, 2)]
        sent = [remote(block, block, ag1_s.at[0], ag1_r.at[0], pair)]
        for i in (1, 2, 3):
            sent.append(remote(block, block, agx_s.at[i, 0], agx_r.at[x, zl], x_dev[i]))
        return sent

    def gather_x_forward(at):
        theirs = mine + 4 * x + 2 * (1 - zl)
        block = v_row[at].at[pl.ds(theirs, 2)]
        remote(block, block, ag1_s.at[0], ag1_r.at[0], pair).wait_recv()
        sent = []
        for i in (1, 2, 3):
            sent.append(remote(block, block, agx_s.at[i, 1], agx_r.at[x, 1 - zl], x_dev[i]))
        whole = v_row[at].at[pl.ds(mine + 4 * x, 4)]
        sent.append(remote(whole, whole, agc_s.at[0], agc_r.at[x], core))
        for copy in sent:
            copy.start()
        return sent

    def gather_x_finish(at):
        sent = []
        for i in (1, 3, 2):
            for e in (0, 1):
                block = v_row[at].at[pl.ds(mine + 4 * x_at[i] + 2 * e, 2)]
                remote(block, block, agx_s.at[i, 0], agx_r.at[x_at[i], e], x_dev[i]).wait_recv()
            whole = v_row[at].at[pl.ds(mine + 4 * x_at[i], 4)]
            copy = remote(whole, whole, agc_s.at[i], agc_r.at[x_at[i]], core)
            copy.start()
            sent.append(copy)
        return sent

    def gather_core_wait(at):
        for i in range(4):
            whole = v_row[at].at[pl.ds(other + 4 * x_at[i], 4)]
            remote(whole, whole, agc_s.at[i], agc_r.at[x_at[i]], core).wait_recv()

    def multiply_up(at, low, high, running):
        def step(j, acc):
            for i in range(UNROLL):
                p = j * UNROLL + i
                part = lax.dot_general(
                    v_col[at][where_i[1, p]], tiles[where_i[0, p]], NT, preferred_element_type=F32
                )
                acc = acc * where_f[0, p] + part
                slots[p] = acc
            return acc

        return lax.fori_loop(low, high, step, running)

    def multiply_down(at, low, high, running):
        def step(j, acc):
            for i in range(UNROLL):
                p = j * UNROLL + i
                part = lax.dot_general(
                    v_row[at][where_i[4, p]], tiles[where_i[3, p]], NN, preferred_element_type=F32
                )
                acc = acc * where_f[2, p] + part
                slots[p] = acc
            return acc

        return lax.fori_loop(low, high, step, running)

    gram_begin()
    by_row = order_by(tile_rows[...], tile_cols[...])
    by_col = order_by(tile_cols[...], tile_rows[...])
    order_i[...] = jnp.zeros_like(order_i)
    order_f[...] = jnp.zeros_like(order_f)
    for i in range(3):
        order_i[i : i + 1, :] = by_row[i]
        order_i[3 + i : 4 + i, :] = by_col[i]
    for i in range(2):
        order_f[i : i + 1, :] = by_row[3 + i]
        order_f[2 + i : 3 + i, :] = by_col[3 + i]
    orders = [
        pltpu.make_async_copy(order_i, where_i, order_sem.at[0]),
        pltpu.make_async_copy(order_f, where_f, order_sem.at[1]),
    ]
    for copy in orders:
        copy.start()
    gram_second(True)
    gram_third(True)
    gram_end(0, True)
    wq[top, :] = dot_high(fact[0, :, 64:128], wq[top, :])
    for copy in orders:
        copy.wait()

    def iterate(at):
        place(at)
        sent = gather_x_begin(at)
        block = v_row[at].at[pl.ds(home, 2)]
        for e in (0, 1):
            there = v_col[at].at[pl.ds(4 * x + 2 * zl, 2)]
            sent.append(remote(block, there, ag1_s.at[1 + e], ag1_r.at[1 + zl], holders[e]))
        for copy in sent[::-1]:
            copy.start()
        gram_begin()
        for e in (0, 1):
            part = v_col[at].at[pl.ds(4 * y + 2 * e, 2)]
            remote(part, part, ag1_s.at[1], ag1_r.at[1 + e], owners[e]).wait_recv()
            for i in (2, 1, 3):
                copy = remote(part, part, agy_s.at[i, e], agy_r.at[y, e], y_dev[i])
                copy.start()
                sent.append(copy)
        sent += gather_x_forward(at)

        if at == 0:
            load.wait()

        for i in (1, 3, 2):
            for e in (0, 1):
                part = v_col[at].at[pl.ds(4 * y_at[i] + 2 * e, 2)]
                remote(part, part, agy_s.at[i, e], agy_r.at[y_at[i], e], y_dev[i]).wait_recv()
        gram_second()

        half = 64 // UNROLL
        zero = jnp.zeros((64, 256), F32)
        running = multiply_up(at, 0, half, zero)
        sent += gather_x_finish(at)
        gram_third()
        multiply_up(at, half, 2 * half, running)
        gather_core_wait(at)

        def pick_up(b, _):
            upper[b] = slots[where_i[2, b]] * where_f[1, b]
            return 0

        lax.fori_loop(0, 32, pick_up, 0)
        for i in (1, 2, 3, 0):
            copy = remote(
                upper.at[pl.ds(other + 4 * x_at[i], 4)], half_in.at[pl.ds(4 * x_at[i], 4)],
                rsc_s.at[i], rsc_r.at[x_at[i]], core,
            )
            copy.start()
            sent.append(copy)
        running = multiply_down(at, 0, half, zero)
        for i in (2, 1, 3, 0):
            q = x_at[i]
            theirs = half_in.at[pl.ds(4 * q, 4)]
            remote(theirs, theirs, rsc_s.at[i], rsc_r.at[q], core).wait_recv()

            def add_half(b, _):
                total = upper[mine + 4 * q + b] + half_in[4 * q + b]
                if i:
                    x_send[4 * i + b] = total.astype(BF16)
                else:
                    upper[mine + 4 * q + b] = total
                return 0

            lax.fori_loop(0, 4, add_half, 0)
            if i:
                copy = remote(
                    x_send.at[pl.ds(4 * i, 4)], x_in.at[pl.ds(4 * (4 - i), 4)],
                    rsx_s.at[i], rsx_r.at[4 - i], x_dev[i],
                )
                copy.start()
                sent.append(copy)
        multiply_down(at, half, 2 * half, running)

        def pick_down(b, _):
            total = slots[where_i[5, b]] * where_f[3, b]
            lower[b] = total
            low_send[b] = total.astype(BF16)
            return 0

        lax.fori_loop(0, 16, pick_down, 0)
        for i in (2, 1, 3):
            copy = remote(
                low_send.at[pl.ds(4 * y_at[i], 4)], y_in.at[pl.ds(4 * (4 - i), 4)],
                rsy_s.at[i], rsy_r.at[4 - i], y_dev[i],
            )
            copy.start()
            sent.append(copy)
        for i in (1, 3, 2):
            part = x_in.at[pl.ds(4 * i, 4)]
            remote(part, part, rsx_s.at[i], rsx_r.at[i], x_dev[i]).wait_recv()

        def add_x(b, _):
            spot = mine + 4 * x + b
            upper[spot] = (
                upper[spot]
                + x_in[4 + b].astype(F32)
                + x_in[8 + b].astype(F32)
                + x_in[12 + b].astype(F32)
            )
            return 0

        lax.fori_loop(0, 4, add_x, 0)
        copy = remote(
            upper.at[pl.ds(mine + 4 * x + 2 * (1 - zl), 2)], row_in, rsf_s.at[0], rsf_r.at[0], pair
        )
        copy.start()
        sent.append(copy)
        gram_end(at)
        for i in (1, 3, 2):
            part = y_in.at[pl.ds(4 * i, 4)]
            remote(part, part, rsy_s.at[i], rsy_r.at[i], y_dev[i]).wait_recv()

        def add_y(b, _):
            col_sum[b] = (
                lower[4 * y + b]
                + y_in[4 + b].astype(F32)
                + y_in[8 + b].astype(F32)
                + y_in[12 + b].astype(F32)
            )
            return 0

        lax.fori_loop(0, 4, add_y, 0)
        for e in (0, 1):
            copy = remote(
                col_sum.at[pl.ds(2 * e, 2)], col_in.at[zh], rsf_s.at[1 + e], rsf_r.at[1 + zh], owners[e]
            )
            copy.start()
            sent.append(copy)

        turned = cross[at]
        inverse = fact[at, :, 64:128]
        old = wq[bottom, :]
        q_new[...] = dot_high(inverse, wq[top, :] - dot_high(turned, old))
        offset[...] = dot_high(inverse, dot_high(turned, applied_old[...]))
        carried[...] = dot_high(fact[at, :, 0:64], old)

        if at > 0:
            alphas[at - 1] = turned.T
            betas[at - 1] = fact[at, :, 0:64]

        wq[bottom, :] = q_new[...]
        remote(row_in, row_in, rsf_s.at[0], rsf_r.at[0], pair).wait_recv()
        for e in (0, 1):
            part = col_in.at[e]
            remote(part, part, rsf_s.at[1 + e], rsf_r.at[1 + e], holders[e]).wait_recv()
        for b in (0, 1):
            spot = pl.ds(256 * b, 256)
            product = upper[home + b] + row_in[b] + col_in[0, b] + col_in[1, b]
            applied = dot_high(inverse, product) - offset[:, spot]
            applied_old[:, spot] = applied
            wq[top, spot] = applied - carried[:, spot]
        for copy in sent:
            copy.wait_send()

    for at in range(ITERS):
        iterate(at)

    place(ITERS)
    sent = gather_x_begin(ITERS)
    for copy in sent:
        copy.start()
    gram_begin()
    sent += gather_x_forward(ITERS)
    gram_second(True)
    sent += gather_x_finish(ITERS)
    gram_third(True)
    mixed = fact[2, :, 64:128]
    parts = [mixed.astype(BF16)]
    for j in (1, 0):
        mixed = -dot_high(dot_high(mixed, cross[j + 1]), fact[j, :, 64:128])
        parts.append(mixed.astype(BF16))
    gather_core_wait(ITERS)

    def old_rows(b, _):
        total = lax.dot_general(parts[0], v_row[2][b], NN, preferred_element_type=F32)
        for j in (1, 0):
            total += lax.dot_general(parts[2 - j], v_row[j][b], NN, preferred_element_type=F32)
        q_row[b] = total.astype(BF16)
        return 0

    lax.fori_loop(0, 32, old_rows, 0)
    gram_end(ITERS, True)
    turned = cross[ITERS]
    alphas[ITERS - 1] = turned.T
    betas[ITERS - 1] = fact[ITERS, :, 0:64]
    inverse = fact[ITERS, :, 64:128]
    high = inverse.astype(BF16)
    low = (inverse - high.astype(F32)).astype(BF16)
    back = dot_high(inverse, turned).astype(BF16)
    for b in range(32):
        block = v_row[ITERS][b]
        total = lax.dot_general(high, block, NN, preferred_element_type=F32)
        total += lax.dot_general(low, block, NN, preferred_element_type=F32)
        total -= lax.dot_general(back, q_row[b], NN, preferred_element_type=F32)
        final[:, 256 * b : 256 * b + 256] = total
    for copy in sent:
        copy.wait_send()


def shards(start_block, tile_values, tile_rows, tile_cols):
    vmem = pl.BlockSpec(memory_space=pltpu.VMEM)
    hbm = pl.BlockSpec(memory_space=pl.ANY)
    dma = pltpu.SemaphoreType.DMA
    alphas, betas, final = pl.pallas_call(
        kernel,
        out_shape=[
            jax.ShapeDtypeStruct((ITERS, 64, 64), F32),
            jax.ShapeDtypeStruct((ITERS, 64, 64), F32),
            jax.ShapeDtypeStruct((64, 8192), F32),
        ],
        in_specs=[vmem, vmem, hbm, hbm],
        out_specs=[vmem] * 3,
        scratch_shapes=[
            pltpu.VMEM((128, 256, 256), BF16),
            pltpu.VMEM((128, 64, 256), F32),
            *[pltpu.VMEM((32, 64, 256), BF16)] * 4,
            *[pltpu.VMEM((16, 64, 256), BF16)] * 3,
            pltpu.VMEM((32, 64, 256), F32),
            pltpu.VMEM((16, 64, 256), F32),
            pltpu.VMEM((16, 64, 256), BF16),
            pltpu.VMEM((16, 64, 256), F32),
            pltpu.VMEM((16, 64, 256), BF16),
            pltpu.VMEM((16, 64, 256), BF16),
            pltpu.VMEM((16, 64, 256), BF16),
            pltpu.VMEM((2, 64, 256), F32),
            pltpu.VMEM((2, 2, 64, 256), F32),
            pltpu.VMEM((4, 64, 256), F32),
            pltpu.VMEM((128, 512), F32),
            pltpu.VMEM((64, 512), F32),
            pltpu.VMEM((64, 512), F32),
            pltpu.VMEM((64, 512), F32),
            pltpu.VMEM((64, 512), F32),
            pltpu.VMEM((4, 64, 128), F32),
            pltpu.VMEM((4, 64, 64), F32),
            pltpu.VMEM((32, 64, 256), BF16),
            pltpu.VMEM((16, 4, 128), F32),
            pltpu.VMEM((16, 4, 128), F32),
            pltpu.VMEM((8, 4, 128), F32),
            pltpu.VMEM((8, 4, 128), F32),
            pltpu.VMEM((16, 4, 128), F32),
            pltpu.VMEM((8, 128), jnp.int32),
            pltpu.VMEM((8, 128), F32),
            pltpu.SMEM((8, 128), jnp.int32),
            pltpu.SMEM((8, 128), F32),
            dma, dma, dma((2,)),
            dma((3,)), dma((3,)), dma((4, 2)), dma((4, 2)), dma((4, 2)), dma((4, 2)),
            dma((4,)), dma((4,)),
            dma((4,)), dma((4,)), dma((4,)), dma((4,)), dma((4,)), dma((4,)), dma((3,)), dma((3,)),
            dma((16,)), dma((16,)), dma((8,)), dma((8,)), dma((8,)), dma((8,)), dma((16,)), dma((16,)),
        ],
        compiler_params=pltpu.CompilerParams(
            collective_id=0, has_side_effects=True, vmem_limit_bytes=56 * 1024 * 1024
        ),
    )(tile_rows[0], tile_cols[0], start_block, tile_values[0, 0])
    total_rows = start_block.shape[1] * lax.axis_size("row")
    return alphas, betas, final * math.sqrt(total_rows)


def solution(mesh):
    in_specs = (
        P(None, "row"),
        P("row", "col", None, None, None),
        P("row", "col", None),
        P("row", "col", None),
    )
    out_specs = (P(), P(), P(None, "row"))
    return jax.shard_map(shards, mesh=mesh, in_specs=in_specs, out_specs=out_specs, check_vma=False)
```

time: 282 us -> 239 us (0.85)
  Pallas kernels: 268 us -> 233 us
  other arithmetic: 10.5 us -> 3.1 us
    pallas_call x1, Pallas kernels: 268 us -> 233 us  [shards(): pl.pallas_call(kernel, out_shape=[jax.ShapeDtypeStruct((ITERS, 64, 64), F...]
    reduce_sum x5 -> x0, other arithmetic: 3.27 us -> none  [the longest x2 1.55 us: order_by(): upto = jnp.sum((keys[None, :] <= block[:, None]).astype(jnp.int32), axis=1)]
    mul x0 -> x1, other arithmetic: none -> 3.1 us  [shards(): return (alphas, betas, final * math.sqrt(total_rows))]
where the time goes in v2:
time: 239 us; the launch traced here: 238 us
  Pallas kernels  233 us (97%)
  other arithmetic  3.1 us (1%)
    pallas_call x1, Pallas kernels, shards(): pl.pallas_call(kernel, out_shape=[jax.ShapeDtypeStruct((ITERS, 64, 64), F...  233 us

profile of v2, /device:TPU:1, one launch (start us, length us, event | category | flops | bytes accessed | tf_op | source)
XLA Modules:
  0.0 237.9 jit_solution(2453732149458623238)
XLA Ops:
  0.6 232.9 %shard_map.67 = (f32[3,64,64]{2,1,0:T(8,128)}, f32[3,64,64]{2,1,0:T(8,128)}, f32[64,8192]{1,0:T(8,128)}) custom-call(s32[1,128]{1,0:T(1,128)} %bitcast.4, s32[1,128]{1,0:T(1,128)} %bitcast.5, f32[64,8192]{1,0:T(8,128)} %start.1, bf16[128,256,256]{2,1,0:T(8,128)(2,1)} %bitcast.3), custom_call_target="tpu_custom_call" | custom-call | tf_op jit(solution)/shard_map/pallas_call | solution.py:492
  233.5 0.0 copy-start.1
  233.5 0.0 copy-start
  233.5 3.1 %broadcast_multiply_fusion = f32[64,8192]{1,0:T(8,128)} fusion(f32[64,8192]{1,0:T(8,128)} %get-tuple-element.8), kind=kLoop, calls=%fused_computation | loop fusion | flops 524288 | bytes 4194304 | tf_op jit(solution)/shard_map/mul | solution.py:544
  236.6 0.0 copy-done.1
  236.6 0.6 copy.9
  237.3 0.0 copy-done
  237.3 0.6 copy.10
Async XLA Ops:
  233.5 3.1 %copy-start.1 = (f32[3,64,64]{2,1,0:T(8,128)S(1)}, f32[3,64,64]{2,1,0:T(8,128)}, u32[]{:S(2)}) copy-start(f32[3,64,64]{2,1,0:T(8,128)} %get-tuple-element.12) | copy-start | bytes 147460
  233.5 3.8 %copy-start = (f32[3,64,64]{2,1,0:T(8,128)S(1)}, f32[3,64,64]{2,1,0:T(8,128)}, u32[]{:S(2)}) copy-start(f32[3,64,64]{2,1,0:T(8,128)} %get-tuple-element.13) | copy-start | bytes 147460

commit v3 on v2

--- a/solution.py
+++ b/solution.py
@@ -15,6 +15,7 @@
 NT = (((1,), (1,)), ((), ()))
 NN = (((1,), (0,)), ((), ()))
 UNROLL = 16
+OTHERS = ((0, 2), (0, 1), (0, 3), (1, 0), (1, 2), (1, 1), (1, 3))
 
 
 def dot_high(a, b, dims=NN):
@@ -70,36 +71,53 @@
     tile_rows, tile_cols, start, tiles_hbm,
     alphas, betas, final,
     tiles, slots, v_r0, v_r1, v_r2, v_r3, v_c0, v_c1, v_c2, upper, lower, low_send,
-    half_in, x_send, x_in, y_in, row_in, col_in, col_sum,
+    half_in, x_send, x_in, y_in, col_in, col_sum,
     wq, q_new, applied_old, offset, carried, fact, cross, q_row,
-    g_send, g_one, g_two, g_two_alone, g_three,
+    start_row, g_first, g_send, g_one, g_two, g_two_alone, g_three,
     order_i, order_f, where_i, where_f,
     load_sem, start_sem, order_sem,
-    ag1_s, ag1_r, agx_s, agx_r, agy_s, agy_r, agc_s, agc_r,
-    rsc_s, rsc_r, rsx_s, rsx_r, rsy_s, rsy_r, rsf_s, rsf_r,
-    g1_s, g1_r, g2_s, g2_r, g2l_s, g2l_r, g3_s, g3_r,
+    agp_s, agp_r, agx_s, agx_r, agy_s, agy_r, agc_s, agc_r,
+    rsc_s, rsc_r, rsx_s, rsx_r, rsy_s, rsy_r, rsp_s, rsp_r,
+    g0_s, g0_r, g1_s, g1_r, g2_s, g2_r, g2l_s, g2l_r, g3_s, g3_r,
 ):
     r = lax.axis_index("row")
     c = lax.axis_index("col")
     zh, y = r // 4, r % 4
     x, zl, k = c // 4, (c // 2) % 2, c % 2
     core = (r, c + 1 - 2 * k)
-    pair = (r, c + 2 - 4 * zl)
     x_at = [(x + i) % 4 for i in range(4)]
-    y_at = [(y + i) % 4 for i in range(4)]
-    x_dev = [(r, i * 4 + zl * 2 + k) for i in x_at]
-    y_dev = [(zh * 4 + i, c) for i in y_at]
-    holders = [(e * 4 + x, (zh * 2 + y // 2) * 4 + (y % 2) * 2 + (1 - k)) for e in (0, 1)]
-    owners = [(2 * x + zl, y * 4 + e * 2 + (1 - k)) for e in (0, 1)]
+    owner = (2 * x + zl, ((x + y + 2 * k) % 4) * 4 + zh * 2 + (1 - k))
+    holder_x = zh * 2 + y // 2
+    holder = (
+        zl * 4 + (x - holder_x - 2 * (1 - k) + 8) % 4,
+        holder_x * 4 + (y % 2) * 2 + (1 - k),
+    )
+
+    def x_device(a, i):
+        return (r, x_at[i] * 4 + ((zl + a) % 2) * 2 + k)
+
+    def y_device(a, i):
+        return (((zh + a) % 2) * 4 + (y + i) % 4, c)
+
+    def x_spot(a, i):
+        return 4 * x_at[i] + 2 * ((zl + a) % 2)
+
+    def y_spot(a, i):
+        return 4 * ((x + y + i + 2 * k) % 4) + 2 * ((zh + a) % 2)
+
+    def slot(a, i):
+        return a * 4 + i
+
+    def slot_there(a, i):
+        return a * 4 + (4 - i) % 4
+
     mine = (1 - k) * 16
     other = k * 16
     home = mine + 4 * x + 2 * zl
     top, bottom = pl.ds(0, 64), pl.ds(64, 64)
     v_row, v_col = (v_r0, v_r1, v_r2, v_r3), (v_c0, v_c1, v_c2)
 
-    first = pltpu.make_async_copy(
-        start.at[:, pl.ds(pl.multiple_of(home * 256, 512), 512)], wq.at[top, :], start_sem
-    )
+    first = pltpu.make_async_copy(start, start_row, start_sem)
     first.start()
     load = pltpu.make_async_copy(tiles_hbm, tiles, load_sem)
     load.start()
@@ -116,12 +134,10 @@
 
     lax.fori_loop(1, 16, greet_row, 0)
     lax.fori_loop(1, 8, greet_col, 0)
-    for device in holders + owners:
+    for device in (owner, holder):
         pl.semaphore_signal(barrier, inc=1, device_id=device, device_id_type=MESH)
     wq[bottom, :] = jnp.zeros((64, 512), F32)
     applied_old[...] = jnp.zeros_like(applied_old)
-    first.wait()
-    pl.semaphore_wait(barrier, 26)
 
     def remote(src, dst, s, d, device):
         return pltpu.make_async_remote_copy(
@@ -185,49 +201,42 @@
         turned = fact[at, :, 64:128]
         cross[at] = turned
         fact[at, :, 0:64] = fact[at, :, 0:64] - dot_high(turned, turned, NT)
+        factorize(at)
+        each(16, lambda i: one(i).wait_send())
+        each(8, lambda i: two(i, last).wait_send())
+        each(16, lambda i: three(i).wait_send())
+
+    def factorize(at):
         eye_r = lax.broadcasted_iota(jnp.int32, (64, 64), 0)
         eye_c = lax.broadcasted_iota(jnp.int32, (64, 64), 1)
         fact[at, :, 64:128] = (eye_r == eye_c).astype(F32)
         done = factor_rows([fact[at, 8 * i : 8 * i + 8, :] for i in range(8)])
         for i in range(8):
             fact[at, 8 * i : 8 * i + 8, :] = done[i]
-        each(16, lambda i: one(i).wait_send())
-        each(8, lambda i: two(i, last).wait_send())
-        each(16, lambda i: three(i).wait_send())
 
     def place(at):
         rounded = wq[top, :].astype(BF16)
         v_row[at][home] = rounded[:, 0:256]
         v_row[at][home + 1] = rounded[:, 256:512]
 
-    def gather_x_begin(at):
+    def gather_rows_begin(at):
         block = v_row[at].at[pl.ds(home, 2)]
-        sent = [remote(block, block, ag1_s.at[0], ag1_r.at[0], pair)]
-        for i in (1, 2, 3):
-            sent.append(remote(block, block, agx_s.at[i, 0], agx_r.at[x, zl], x_dev[i]))
-        return sent
-
-    def gather_x_forward(at):
-        theirs = mine + 4 * x + 2 * (1 - zl)
-        block = v_row[at].at[pl.ds(theirs, 2)]
-        remote(block, block, ag1_s.at[0], ag1_r.at[0], pair).wait_recv()
+        return [
+            remote(block, block, agx_s.at[slot(a, i)], agx_r.at[slot_there(a, i)], x_device(a, i))
+            for a, i in OTHERS
+        ]
+
+    def gather_rows_finish(at):
         sent = []
-        for i in (1, 2, 3):
-            sent.append(remote(block, block, agx_s.at[i, 1], agx_r.at[x, 1 - zl], x_dev[i]))
-        whole = v_row[at].at[pl.ds(mine + 4 * x, 4)]
-        sent.append(remote(whole, whole, agc_s.at[0], agc_r.at[x], core))
-        for copy in sent:
-            copy.start()
-        return sent
-
-    def gather_x_finish(at):
-        sent = []
-        for i in (1, 3, 2):
-            for e in (0, 1):
-                block = v_row[at].at[pl.ds(mine + 4 * x_at[i] + 2 * e, 2)]
-                remote(block, block, agx_s.at[i, 0], agx_r.at[x_at[i], e], x_dev[i]).wait_recv()
+        for i in (0, 1, 3, 2):
+            for a in (0, 1):
+                if (a, i) != (0, 0):
+                    block = v_row[at].at[pl.ds(mine + x_spot(a, i), 2)]
+                    remote(
+                        block, block, agx_s.at[slot(a, i)], agx_r.at[slot(a, i)], x_device(a, i)
+                    ).wait_recv()
             whole = v_row[at].at[pl.ds(mine + 4 * x_at[i], 4)]
-            copy = remote(whole, whole, agc_s.at[i], agc_r.at[x_at[i]], core)
+            copy = remote(whole, whole, agc_s.at[i], agc_r.at[i], core)
             copy.start()
             sent.append(copy)
         return sent
@@ -235,7 +244,7 @@
     def gather_core_wait(at):
         for i in range(4):
             whole = v_row[at].at[pl.ds(other + 4 * x_at[i], 4)]
-            remote(whole, whole, agc_s.at[i], agc_r.at[x_at[i]], core).wait_recv()
+            remote(whole, whole, agc_s.at[i], agc_r.at[i], core).wait_recv()
 
     def multiply_up(at, low, high, running):
         def step(j, acc):
@@ -263,7 +272,33 @@
 
         return lax.fori_loop(low, high, step, running)
 
-    gram_begin()
+    first.wait()
+
+    def start_gram(i, acc):
+        block = start_row[:, pl.ds(pl.multiple_of(i * 512, 512), 512)]
+        high = block.astype(BF16)
+        rest = block - high.astype(F32)
+        middle = rest.astype(BF16)
+        low = (rest - middle.astype(F32)).astype(BF16)
+        terms = jnp.concatenate([high, middle, low], axis=0)
+        return acc + lax.dot_general(terms, terms, NT, preferred_element_type=F32)
+
+    gram = lax.fori_loop(0, 16, start_gram, jnp.zeros((192, 192), F32))
+    gram = gram[0:64, :] + gram[64:128, :] + gram[128:192, :]
+    gram = gram[:, 0:64] + gram[:, 64:128] + gram[:, 128:192]
+    g_first[r, :, 0:64] = gram[0:32, :]
+    g_first[r, :, 64:128] = gram[32:64, :]
+    pl.semaphore_wait(barrier, 24)
+
+    def zero_out(i):
+        p = (r + i) % 8
+        return remote(g_first.at[r], g_first.at[r], g0_s.at[i], g0_r.at[r], (p, c))
+
+    def zero_in(i):
+        p = (r + i) % 8
+        return remote(g_first.at[p], g_first.at[p], g0_s.at[i], g0_r.at[p], (p, c))
+
+    each(8, lambda i: zero_out(i).start())
     by_row = order_by(tile_rows[...], tile_cols[...])
     by_col = order_by(tile_cols[...], tile_rows[...])
     order_i[...] = jnp.zeros_like(order_i)
@@ -280,84 +315,40 @@
     ]
     for copy in orders:
         copy.start()
-    gram_second(True)
-    gram_third(True)
-    gram_end(0, True)
-    wq[top, :] = dot_high(fact[0, :, 64:128], wq[top, :])
+    each(8, lambda i: zero_in(i).wait_recv())
+    total = jnp.sum(g_first[...], axis=0)
+    fact[0, 0:32, 0:64] = total[:, 0:64]
+    fact[0, 32:64, 0:64] = total[:, 64:128]
+    factorize(0)
+    begin = start_row[:, pl.ds(pl.multiple_of(home * 256, 512), 512)]
+    wq[top, :] = dot_high(fact[0, :, 64:128], begin)
     for copy in orders:
         copy.wait()
+    each(8, lambda i: zero_out(i).wait_send())
 
     def iterate(at):
+        bank = at % 2
         place(at)
-        sent = gather_x_begin(at)
         block = v_row[at].at[pl.ds(home, 2)]
-        for e in (0, 1):
-            there = v_col[at].at[pl.ds(4 * x + 2 * zl, 2)]
-            sent.append(remote(block, there, ag1_s.at[1 + e], ag1_r.at[1 + zl], holders[e]))
-        for copy in sent[::-1]:
+        there = v_col[at].at[pl.ds(4 * x + 2 * zl, 2)]
+        sent = [remote(block, there, agp_s, agp_r, holder)]
+        sent += gather_rows_begin(at)
+        for copy in sent:
             copy.start()
         gram_begin()
-        for e in (0, 1):
-            part = v_col[at].at[pl.ds(4 * y + 2 * e, 2)]
-            remote(part, part, ag1_s.at[1], ag1_r.at[1 + e], owners[e]).wait_recv()
-            for i in (2, 1, 3):
-                copy = remote(part, part, agy_s.at[i, e], agy_r.at[y, e], y_dev[i])
-                copy.start()
-                sent.append(copy)
-        sent += gather_x_forward(at)
-
+        part = v_col[at].at[pl.ds(y_spot(0, 0), 2)]
+        remote(part, part, agp_s, agp_r, owner).wait_recv()
+        for a, i in OTHERS:
+            copy = remote(part, part, agy_s.at[slot(a, i)], agy_r.at[slot_there(a, i)], y_device(a, i))
+            copy.start()
+            sent.append(copy)
+        sent += gather_rows_finish(at)
         if at == 0:
             load.wait()
-
-        for i in (1, 3, 2):
-            for e in (0, 1):
-                part = v_col[at].at[pl.ds(4 * y_at[i] + 2 * e, 2)]
-                remote(part, part, agy_s.at[i, e], agy_r.at[y_at[i], e], y_dev[i]).wait_recv()
-        gram_second()
-
-        half = 64 // UNROLL
+        gather_core_wait(at)
+
         zero = jnp.zeros((64, 256), F32)
-        running = multiply_up(at, 0, half, zero)
-        sent += gather_x_finish(at)
-        gram_third()
-        multiply_up(at, half, 2 * half, running)
-        gather_core_wait(at)
-
-        def pick_up(b, _):
-            upper[b] = slots[where_i[2, b]] * where_f[1, b]
-            return 0
-
-        lax.fori_loop(0, 32, pick_up, 0)
-        for i in (1, 2, 3, 0):
-            copy = remote(
-                upper.at[pl.ds(other + 4 * x_at[i], 4)], half_in.at[pl.ds(4 * x_at[i], 4)],
-                rsc_s.at[i], rsc_r.at[x_at[i]], core,
-            )
-            copy.start()
-            sent.append(copy)
-        running = multiply_down(at, 0, half, zero)
-        for i in (2, 1, 3, 0):
-            q = x_at[i]
-            theirs = half_in.at[pl.ds(4 * q, 4)]
-            remote(theirs, theirs, rsc_s.at[i], rsc_r.at[q], core).wait_recv()
-
-            def add_half(b, _):
-                total = upper[mine + 4 * q + b] + half_in[4 * q + b]
-                if i:
-                    x_send[4 * i + b] = total.astype(BF16)
-                else:
-                    upper[mine + 4 * q + b] = total
-                return 0
-
-            lax.fori_loop(0, 4, add_half, 0)
-            if i:
-                copy = remote(
-                    x_send.at[pl.ds(4 * i, 4)], x_in.at[pl.ds(4 * (4 - i), 4)],
-                    rsx_s.at[i], rsx_r.at[4 - i], x_dev[i],
-                )
-                copy.start()
-                sent.append(copy)
-        multiply_down(at, half, 2 * half, running)
+        multiply_down(at, 0, 128 // UNROLL, zero)
 
         def pick_down(b, _):
             total = slots[where_i[5, b]] * where_f[3, b]
@@ -366,54 +357,72 @@
             return 0
 
         lax.fori_loop(0, 16, pick_down, 0)
-        for i in (2, 1, 3):
+        for a, i in OTHERS:
             copy = remote(
-                low_send.at[pl.ds(4 * y_at[i], 4)], y_in.at[pl.ds(4 * (4 - i), 4)],
-                rsy_s.at[i], rsy_r.at[4 - i], y_dev[i],
+                low_send.at[pl.ds(y_spot(a, i), 2)], y_in.at[bank, pl.ds(2 * slot_there(a, i), 2)],
+                rsy_s.at[slot(a, i)], rsy_r.at[bank, slot_there(a, i)], y_device(a, i),
             )
             copy.start()
             sent.append(copy)
-        for i in (1, 3, 2):
-            part = x_in.at[pl.ds(4 * i, 4)]
-            remote(part, part, rsx_s.at[i], rsx_r.at[i], x_dev[i]).wait_recv()
-
-        def add_x(b, _):
-            spot = mine + 4 * x + b
-            upper[spot] = (
-                upper[spot]
-                + x_in[4 + b].astype(F32)
-                + x_in[8 + b].astype(F32)
-                + x_in[12 + b].astype(F32)
+        for a, i in OTHERS:
+            part = v_col[at].at[pl.ds(y_spot(a, i), 2)]
+            remote(
+                part, part, agy_s.at[slot(a, i)], agy_r.at[slot(a, i)], y_device(a, i)
+            ).wait_recv()
+        gram_second()
+
+        half = 64 // UNROLL
+        running = multiply_up(at, 0, half, zero)
+        gram_third()
+        multiply_up(at, half, 2 * half, running)
+
+        def pick_up(b, _):
+            upper[b] = slots[where_i[2, b]] * where_f[1, b]
+            return 0
+
+        lax.fori_loop(0, 32, pick_up, 0)
+        for i in (2, 1, 3, 0):
+            copy = remote(
+                upper.at[pl.ds(other + 4 * x_at[i], 4)], half_in.at[pl.ds(4 * x_at[i], 4)],
+                rsc_s.at[i], rsc_r.at[i], core,
             )
-            return 0
-
-        lax.fori_loop(0, 4, add_x, 0)
-        copy = remote(
-            upper.at[pl.ds(mine + 4 * x + 2 * (1 - zl), 2)], row_in, rsf_s.at[0], rsf_r.at[0], pair
-        )
+            copy.start()
+            sent.append(copy)
+        for i in (2, 1, 3, 0):
+            q = x_at[i]
+            theirs = half_in.at[pl.ds(4 * q, 4)]
+            remote(theirs, theirs, rsc_s.at[i], rsc_r.at[i], core).wait_recv()
+
+            def add_half(b, _):
+                total = upper[mine + 4 * q + b] + half_in[4 * q + b]
+                x_send[4 * q + b] = total.astype(BF16)
+                if i == 0:
+                    upper[mine + 4 * q + b] = total
+                return 0
+
+            lax.fori_loop(0, 4, add_half, 0)
+            for a in (1, 0):
+                if (a, i) != (0, 0):
+                    copy = remote(
+                        x_send.at[pl.ds(x_spot(a, i), 2)], x_in.at[pl.ds(2 * slot_there(a, i), 2)],
+                        rsx_s.at[slot(a, i)], rsx_r.at[slot_there(a, i)], x_device(a, i),
+                    )
+                    copy.start()
+                    sent.append(copy)
+        for a, i in OTHERS:
+            part = y_in.at[bank, pl.ds(2 * slot(a, i), 2)]
+            remote(
+                part, part, rsy_s.at[slot(a, i)], rsy_r.at[bank, slot(a, i)], y_device(a, i)
+            ).wait_recv()
+        for b in (0, 1):
+            total = lower[y_spot(0, 0) + b]
+            for a, i in OTHERS:
+                total = total + y_in[bank, 2 * slot(a, i) + b].astype(F32)
+            col_sum[b] = total
+        copy = remote(col_sum, col_in, rsp_s, rsp_r, owner)
         copy.start()
         sent.append(copy)
         gram_end(at)
-        for i in (1, 3, 2):
-            part = y_in.at[pl.ds(4 * i, 4)]
-            remote(part, part, rsy_s.at[i], rsy_r.at[i], y_dev[i]).wait_recv()
-
-        def add_y(b, _):
-            col_sum[b] = (
-                lower[4 * y + b]
-                + y_in[4 + b].astype(F32)
-                + y_in[8 + b].astype(F32)
-                + y_in[12 + b].astype(F32)
-            )
-            return 0
-
-        lax.fori_loop(0, 4, add_y, 0)
-        for e in (0, 1):
-            copy = remote(
-                col_sum.at[pl.ds(2 * e, 2)], col_in.at[zh], rsf_s.at[1 + e], rsf_r.at[1 + zh], owners[e]
-            )
-            copy.start()
-            sent.append(copy)
 
         turned = cross[at]
         inverse = fact[at, :, 64:128]
@@ -421,19 +430,24 @@
         q_new[...] = dot_high(inverse, wq[top, :] - dot_high(turned, old))
         offset[...] = dot_high(inverse, dot_high(turned, applied_old[...]))
         carried[...] = dot_high(fact[at, :, 0:64], old)
-
         if at > 0:
             alphas[at - 1] = turned.T
             betas[at - 1] = fact[at, :, 0:64]
-
         wq[bottom, :] = q_new[...]
-        remote(row_in, row_in, rsf_s.at[0], rsf_r.at[0], pair).wait_recv()
-        for e in (0, 1):
-            part = col_in.at[e]
-            remote(part, part, rsf_s.at[1 + e], rsf_r.at[1 + e], holders[e]).wait_recv()
+        for a, i in OTHERS:
+            part = x_in.at[pl.ds(2 * slot(a, i), 2)]
+            remote(
+                part, part, rsx_s.at[slot(a, i)], rsx_r.at[slot(a, i)], x_device(a, i)
+            ).wait_recv()
+        for b in (0, 1):
+            total = upper[home + b]
+            for a, i in OTHERS:
+                total = total + x_in[2 * slot(a, i) + b].astype(F32)
+            upper[home + b] = total
+        remote(col_sum, col_in, rsp_s, rsp_r, holder).wait_recv()
         for b in (0, 1):
             spot = pl.ds(256 * b, 256)
-            product = upper[home + b] + row_in[b] + col_in[0, b] + col_in[1, b]
+            product = upper[home + b] + col_in[b]
             applied = dot_high(inverse, product) - offset[:, spot]
             applied_old[:, spot] = applied
             wq[top, spot] = applied - carried[:, spot]
@@ -444,13 +458,12 @@
         iterate(at)
 
     place(ITERS)
-    sent = gather_x_begin(ITERS)
+    sent = gather_rows_begin(ITERS)
+    gram_begin()
     for copy in sent:
         copy.start()
-    gram_begin()
-    sent += gather_x_forward(ITERS)
     gram_second(True)
-    sent += gather_x_finish(ITERS)
+    sent += gather_rows_finish(ITERS)
     gram_third(True)
     mixed = fact[2, :, 64:128]
     parts = [mixed.astype(BF16)]
@@ -509,10 +522,9 @@
             pltpu.VMEM((16, 64, 256), F32),
             pltpu.VMEM((16, 64, 256), BF16),
             pltpu.VMEM((16, 64, 256), BF16),
-            pltpu.VMEM((16, 64, 256), BF16),
+            pltpu.VMEM((2, 16, 64, 256), BF16),
             pltpu.VMEM((2, 64, 256), F32),
-            pltpu.VMEM((2, 2, 64, 256), F32),
-            pltpu.VMEM((4, 64, 256), F32),
+            pltpu.VMEM((2, 64, 256), F32),
             pltpu.VMEM((128, 512), F32),
             pltpu.VMEM((64, 512), F32),
             pltpu.VMEM((64, 512), F32),
@@ -521,6 +533,8 @@
             pltpu.VMEM((4, 64, 128), F32),
             pltpu.VMEM((4, 64, 64), F32),
             pltpu.VMEM((32, 64, 256), BF16),
+            pltpu.VMEM((64, 8192), F32),
+            pltpu.VMEM((8, 32, 128), F32),
             pltpu.VMEM((16, 4, 128), F32),
             pltpu.VMEM((16, 4, 128), F32),
             pltpu.VMEM((8, 4, 128), F32),
@@ -531,9 +545,9 @@
             pltpu.SMEM((8, 128), jnp.int32),
             pltpu.SMEM((8, 128), F32),
             dma, dma, dma((2,)),
-            dma((3,)), dma((3,)), dma((4, 2)), dma((4, 2)), dma((4, 2)), dma((4, 2)),
-            dma((4,)), dma((4,)),
-            dma((4,)), dma((4,)), dma((4,)), dma((4,)), dma((4,)), dma((4,)), dma((3,)), dma((3,)),
+            dma, dma, dma((8,)), dma((8,)), dma((8,)), dma((8,)), dma((4,)), dma((4,)),
+            dma((4,)), dma((4,)), dma((8,)), dma((8,)), dma((8,)), dma((2, 8)), dma, dma,
+            dma((8,)), dma((8,)),
             dma((16,)), dma((16,)), dma((8,)), dma((8,)), dma((8,)), dma((8,)), dma((16,)), dma((16,)),
         ],
         compiler_params=pltpu.CompilerParams(

time: 239 us -> 187 us (0.78)
  Pallas kernels: 233 us -> 182 us
    pallas_call x1, Pallas kernels: 233 us -> 182 us  [shards(): pl.pallas_call(kernel, out_shape=[jax.ShapeDtypeStruct((ITERS, 64, 64), F...]
where the time goes in v3:
time: 187 us
  Pallas kernels  182 us (97%)
  other arithmetic  3.1 us (2%)
    pallas_call x1, Pallas kernels, shards(): pl.pallas_call(kernel, out_shape=[jax.ShapeDtypeStruct((ITERS, 64, 64), F...  182 us

profile of v3, /device:TPU:1, one launch (start us, length us, event | category | flops | bytes accessed | tf_op | source)
XLA Modules:
  0.0 186.8 jit_solution(15251352386185100801)
XLA Ops:
  0.6 181.7 %shard_map.67 = (f32[3,64,64]{2,1,0:T(8,128)}, f32[3,64,64]{2,1,0:T(8,128)}, f32[64,8192]{1,0:T(8,128)}) custom-call(s32[1,128]{1,0:T(1,128)} %bitcast.4, s32[1,128]{1,0:T(1,128)} %bitcast.5, f32[64,8192]{1,0:T(8,128)} %start.1, bf16[128,256,256]{2,1,0:T(8,128)(2,1)} %bitcast.3), custom_call_target="tpu_custom_call" | custom-call | tf_op jit(solution)/shard_map/pallas_call | solution.py:505
  182.4 0.0 copy-start.1
  182.4 0.0 copy-start
  182.4 3.1 %broadcast_multiply_fusion = f32[64,8192]{1,0:T(8,128)} fusion(f32[64,8192]{1,0:T(8,128)} %get-tuple-element.8), kind=kLoop, calls=%fused_computation | loop fusion | flops 524288 | bytes 4194304 | tf_op jit(solution)/shard_map/mul | solution.py:558
  185.5 0.0 copy-done.1
  185.5 0.6 copy.9
  186.1 0.0 copy-done
  186.1 0.6 copy.10
Async XLA Ops:
  182.4 3.1 %copy-start.1 = (f32[3,64,64]{2,1,0:T(8,128)S(1)}, f32[3,64,64]{2,1,0:T(8,128)}, u32[]{:S(2)}) copy-start(f32[3,64,64]{2,1,0:T(8,128)} %get-tuple-element.12) | copy-start | bytes 147460
  182.4 3.8 %copy-start = (f32[3,64,64]{2,1,0:T(8,128)S(1)}, f32[3,64,64]{2,1,0:T(8,128)}, u32[]{:S(2)}) copy-start(f32[3,64,64]{2,1,0:T(8,128)} %get-tuple-element.13) | copy-start | bytes 147460

commit v4 on v3

--- a/solution.py
+++ b/solution.py
@@ -14,7 +14,7 @@
 BF16 = jnp.bfloat16
 NT = (((1,), (1,)), ((), ()))
 NN = (((1,), (0,)), ((), ()))
-UNROLL = 16
+UNROLL = 32
 OTHERS = ((0, 2), (0, 1), (0, 3), (1, 0), (1, 2), (1, 1), (1, 3))
 
 
@@ -69,16 +69,17 @@
 
 def kernel(
     tile_rows, tile_cols, start, tiles_hbm,
-    alphas, betas, final,
+    alphas, betas, factors, last_rows, old_rows,
     tiles, slots, v_r0, v_r1, v_r2, v_r3, v_c0, v_c1, v_c2, upper, lower, low_send,
     half_in, x_send, x_in, y_in, col_in, col_sum,
     wq, q_new, applied_old, offset, carried, fact, cross, q_row,
-    start_row, g_first, g_send, g_one, g_two, g_two_alone, g_three,
+    start_row, start_col, g_first, g_send, g_one, g_two, g_three,
     order_i, order_f, where_i, where_f,
-    load_sem, start_sem, order_sem,
+    load_sem, start_sem, order_sem, out_sem,
+    sp_s, sp_r, sy_s, sy_r,
     agp_s, agp_r, agx_s, agx_r, agy_s, agy_r, agc_s, agc_r,
     rsc_s, rsc_r, rsx_s, rsx_r, rsy_s, rsy_r, rsp_s, rsp_r,
-    g0_s, g0_r, g1_s, g1_r, g2_s, g2_r, g2l_s, g2l_r, g3_s, g3_r,
+    g0_s, g0_r, g1_s, g1_r, g2_s, g2_r, g3_s, g3_r,
 ):
     r = lax.axis_index("row")
     c = lax.axis_index("col")
@@ -120,7 +121,6 @@
     first = pltpu.make_async_copy(start, start_row, start_sem)
     first.start()
     load = pltpu.make_async_copy(tiles_hbm, tiles, load_sem)
-    load.start()
 
     barrier = pltpu.get_barrier_semaphore()
 
@@ -136,8 +136,6 @@
     lax.fori_loop(1, 8, greet_col, 0)
     for device in (owner, holder):
         pl.semaphore_signal(barrier, inc=1, device_id=device, device_id_type=MESH)
-    wq[bottom, :] = jnp.zeros((64, 512), F32)
-    applied_old[...] = jnp.zeros_like(applied_old)
 
     def remote(src, dst, s, d, device):
         return pltpu.make_async_remote_copy(
@@ -159,15 +157,13 @@
         p = (c + i) % 16
         return remote(g_send.at[p], g_one.at[p], g1_s.at[i], g1_r.at[p], (r, p))
 
-    def two(i, last):
+    def two(i, bank):
         p = (r + i) % 8
-        buffer, s, d = (g_two_alone, g2l_s, g2l_r) if last else (g_two, g2_s, g2_r)
-        return remote(buffer.at[r], buffer.at[r], s.at[i], d.at[r], (p, c))
-
-    def two_in(i, last):
+        return remote(g_two.at[bank, r], g_two.at[bank, r], g2_s.at[i], g2_r.at[bank, r], (p, c))
+
+    def two_in(i, bank):
         p = (r + i) % 8
-        buffer, s, d = (g_two_alone, g2l_s, g2l_r) if last else (g_two, g2_s, g2_r)
-        return remote(buffer.at[p], buffer.at[p], s.at[i], d.at[p], (p, c))
+        return remote(g_two.at[bank, p], g_two.at[bank, p], g2_s.at[i], g2_r.at[bank, p], (p, c))
 
     def three(i):
         p = (c + i) % 16
@@ -184,17 +180,17 @@
         each(16, lambda i: one(i).start())
         g_one[c] = g_send[c]
 
-    def gram_second(last=False):
+    def gram_second(bank):
         each(16, lambda i: one_in(i).wait_recv())
-        (g_two_alone if last else g_two)[r] = jnp.sum(g_one[...], axis=0)
-        each(8, lambda i: two(i, last).start())
-
-    def gram_third(last=False):
-        each(8, lambda i: two_in(i, last).wait_recv())
-        g_three[c] = jnp.sum((g_two_alone if last else g_two)[...], axis=0)
+        g_two[bank, r] = jnp.sum(g_one[...], axis=0)
+        each(8, lambda i: two(i, bank).start())
+
+    def gram_third(bank):
+        each(8, lambda i: two_in(i, bank).wait_recv())
+        g_three[c] = jnp.sum(g_two[bank], axis=0)
         each(16, lambda i: three(i).start())
 
-    def gram_end(at, last=False):
+    def gram_end(at):
         each(16, lambda i: three_in(i).wait_recv())
         for i in range(16):
             fact[at, pl.ds(4 * i, 4), :] = g_three[i]
@@ -203,7 +199,7 @@
         fact[at, :, 0:64] = fact[at, :, 0:64] - dot_high(turned, turned, NT)
         factorize(at)
         each(16, lambda i: one(i).wait_send())
-        each(8, lambda i: two(i, last).wait_send())
+        each(8, lambda i: two(i, at - 1).wait_send())
         each(16, lambda i: three(i).wait_send())
 
     def factorize(at):
@@ -273,6 +269,16 @@
         return lax.fori_loop(low, high, step, running)
 
     first.wait()
+    load.start()
+
+    pl.semaphore_wait(barrier, 24)
+    lanes = lambda spot: pl.ds(pl.multiple_of(spot * 256, 512), 512)
+    raw_sent = [
+        remote(
+            start_row.at[:, lanes(home)], start_col.at[:, lanes(4 * x + 2 * zl)], sp_s, sp_r, holder
+        )
+    ]
+    raw_sent[0].start()
 
     def start_gram(i, acc):
         block = start_row[:, pl.ds(pl.multiple_of(i * 512, 512), 512)]
@@ -288,7 +294,6 @@
     gram = gram[:, 0:64] + gram[:, 64:128] + gram[:, 128:192]
     g_first[r, :, 0:64] = gram[0:32, :]
     g_first[r, :, 64:128] = gram[32:64, :]
-    pl.semaphore_wait(barrier, 24)
 
     def zero_out(i):
         p = (r + i) % 8
@@ -315,37 +320,63 @@
     ]
     for copy in orders:
         copy.start()
+    chunk = start_col.at[:, lanes(y_spot(0, 0))]
+    remote(chunk, chunk, sp_s, sp_r, owner).wait_recv()
+    for a, i in OTHERS:
+        copy = remote(chunk, chunk, sy_s.at[slot(a, i)], sy_r.at[slot_there(a, i)], y_device(a, i))
+        copy.start()
+        raw_sent.append(copy)
     each(8, lambda i: zero_in(i).wait_recv())
     total = jnp.sum(g_first[...], axis=0)
     fact[0, 0:32, 0:64] = total[:, 0:64]
     fact[0, 32:64, 0:64] = total[:, 64:128]
     factorize(0)
-    begin = start_row[:, pl.ds(pl.multiple_of(home * 256, 512), 512)]
-    wq[top, :] = dot_high(fact[0, :, 64:128], begin)
+    inverse = fact[0, :, 64:128]
+    wq[top, :] = dot_high(inverse, start_row[:, lanes(home)])
+    high = inverse.astype(BF16)
+    low = (inverse - high.astype(F32)).astype(BF16)
+    left = jnp.concatenate([high, high, low], axis=1)
+
+    def solve(source, target, count):
+        def step(b, _):
+            block = source[:, pl.ds(pl.multiple_of(b * 256, 256), 256)]
+            upper_half = block.astype(BF16)
+            lower_half = (block - upper_half.astype(F32)).astype(BF16)
+            right = jnp.concatenate([upper_half, lower_half, upper_half], axis=0)
+            target[b] = lax.dot_general(left, right, NN, preferred_element_type=F32).astype(BF16)
+            return 0
+
+        lax.fori_loop(0, count, step, 0, unroll=4)
+
+    solve(start_row, v_row[0], 32)
     for copy in orders:
         copy.wait()
     each(8, lambda i: zero_out(i).wait_send())
 
     def iterate(at):
-        bank = at % 2
-        place(at)
-        block = v_row[at].at[pl.ds(home, 2)]
-        there = v_col[at].at[pl.ds(4 * x + 2 * zl, 2)]
-        sent = [remote(block, there, agp_s, agp_r, holder)]
-        sent += gather_rows_begin(at)
-        for copy in sent:
-            copy.start()
-        gram_begin()
-        part = v_col[at].at[pl.ds(y_spot(0, 0), 2)]
-        remote(part, part, agp_s, agp_r, owner).wait_recv()
-        for a, i in OTHERS:
-            copy = remote(part, part, agy_s.at[slot(a, i)], agy_r.at[slot_there(a, i)], y_device(a, i))
-            copy.start()
-            sent.append(copy)
-        sent += gather_rows_finish(at)
+        sent = []
         if at == 0:
             load.wait()
-        gather_core_wait(at)
+        else:
+            place(at)
+            block = v_row[at].at[pl.ds(home, 2)]
+            there = v_col[at].at[pl.ds(4 * x + 2 * zl, 2)]
+            sent.append(remote(block, there, agp_s, agp_r.at[at], holder))
+            sent += gather_rows_begin(at)
+            for copy in sent:
+                copy.start()
+            gram_begin()
+            part = v_col[at].at[pl.ds(y_spot(0, 0), 2)]
+            remote(part, part, agp_s, agp_r.at[at], owner).wait_recv()
+            for a, i in OTHERS:
+                copy = remote(
+                    part, part, agy_s.at[slot(a, i)], agy_r.at[at, slot_there(a, i)], y_device(a, i)
+                )
+                copy.start()
+                sent.append(copy)
+            gram_second(at - 1)
+            sent += gather_rows_finish(at)
+            gather_core_wait(at)
 
         zero = jnp.zeros((64, 256), F32)
         multiply_down(at, 0, 128 // UNROLL, zero)
@@ -359,22 +390,26 @@
         lax.fori_loop(0, 16, pick_down, 0)
         for a, i in OTHERS:
             copy = remote(
-                low_send.at[pl.ds(y_spot(a, i), 2)], y_in.at[bank, pl.ds(2 * slot_there(a, i), 2)],
-                rsy_s.at[slot(a, i)], rsy_r.at[bank, slot_there(a, i)], y_device(a, i),
+                low_send.at[pl.ds(y_spot(a, i), 2)], y_in.at[at, pl.ds(2 * slot_there(a, i), 2)],
+                rsy_s.at[slot(a, i)], rsy_r.at[at, slot_there(a, i)], y_device(a, i),
             )
             copy.start()
             sent.append(copy)
-        for a, i in OTHERS:
-            part = v_col[at].at[pl.ds(y_spot(a, i), 2)]
-            remote(
-                part, part, agy_s.at[slot(a, i)], agy_r.at[slot(a, i)], y_device(a, i)
-            ).wait_recv()
-        gram_second()
-
-        half = 64 // UNROLL
-        running = multiply_up(at, 0, half, zero)
-        gram_third()
-        multiply_up(at, half, 2 * half, running)
+        if at == 0:
+            for a, i in OTHERS:
+                part = start_col.at[:, lanes(y_spot(a, i))]
+                remote(
+                    part, part, sy_s.at[slot(a, i)], sy_r.at[slot(a, i)], y_device(a, i)
+                ).wait_recv()
+            solve(start_col, v_col[0], 16)
+        else:
+            gram_third(at - 1)
+            for a, i in OTHERS:
+                part = v_col[at].at[pl.ds(y_spot(a, i), 2)]
+                remote(
+                    part, part, agy_s.at[slot(a, i)], agy_r.at[at, slot(a, i)], y_device(a, i)
+                ).wait_recv()
+        multiply_up(at, 0, 128 // UNROLL, zero)
 
         def pick_up(b, _):
             upper[b] = slots[where_i[2, b]] * where_f[1, b]
@@ -410,30 +445,31 @@
                     copy.start()
                     sent.append(copy)
         for a, i in OTHERS:
-            part = y_in.at[bank, pl.ds(2 * slot(a, i), 2)]
+            part = y_in.at[at, pl.ds(2 * slot(a, i), 2)]
             remote(
-                part, part, rsy_s.at[slot(a, i)], rsy_r.at[bank, slot(a, i)], y_device(a, i)
+                part, part, rsy_s.at[slot(a, i)], rsy_r.at[at, slot(a, i)], y_device(a, i)
             ).wait_recv()
         for b in (0, 1):
             total = lower[y_spot(0, 0) + b]
             for a, i in OTHERS:
-                total = total + y_in[bank, 2 * slot(a, i) + b].astype(F32)
+                total = total + y_in[at, 2 * slot(a, i) + b].astype(F32)
             col_sum[b] = total
         copy = remote(col_sum, col_in, rsp_s, rsp_r, owner)
         copy.start()
         sent.append(copy)
-        gram_end(at)
-
-        turned = cross[at]
-        inverse = fact[at, :, 64:128]
-        old = wq[bottom, :]
-        q_new[...] = dot_high(inverse, wq[top, :] - dot_high(turned, old))
-        offset[...] = dot_high(inverse, dot_high(turned, applied_old[...]))
-        carried[...] = dot_high(fact[at, :, 0:64], old)
-        if at > 0:
+        if at == 0:
+            wq[bottom, :] = wq[top, :]
+        else:
+            gram_end(at)
+            turned = cross[at]
+            inverse = fact[at, :, 64:128]
+            old = wq[bottom, :]
+            q_new[...] = dot_high(inverse, wq[top, :] - dot_high(turned, old))
+            offset[...] = dot_high(inverse, dot_high(turned, applied_old[...]))
+            carried[...] = dot_high(fact[at, :, 0:64], old)
             alphas[at - 1] = turned.T
             betas[at - 1] = fact[at, :, 0:64]
-        wq[bottom, :] = q_new[...]
+            wq[bottom, :] = q_new[...]
         for a, i in OTHERS:
             part = x_in.at[pl.ds(2 * slot(a, i), 2)]
             remote(
@@ -448,69 +484,85 @@
         for b in (0, 1):
             spot = pl.ds(256 * b, 256)
             product = upper[home + b] + col_in[b]
-            applied = dot_high(inverse, product) - offset[:, spot]
-            applied_old[:, spot] = applied
-            wq[top, spot] = applied - carried[:, spot]
+            if at == 0:
+                applied_old[:, spot] = product
+                wq[top, spot] = product
+            else:
+                applied = dot_high(inverse, product) - offset[:, spot]
+                applied_old[:, spot] = applied
+                wq[top, spot] = applied - carried[:, spot]
         for copy in sent:
             copy.wait_send()
 
     for at in range(ITERS):
         iterate(at)
+    for copy in raw_sent:
+        copy.wait_send()
 
     place(ITERS)
     sent = gather_rows_begin(ITERS)
     gram_begin()
     for copy in sent:
         copy.start()
-    gram_second(True)
+    gram_second(ITERS - 1)
     sent += gather_rows_finish(ITERS)
-    gram_third(True)
+    gram_third(ITERS - 1)
     mixed = fact[2, :, 64:128]
     parts = [mixed.astype(BF16)]
-    for j in (1, 0):
-        mixed = -dot_high(dot_high(mixed, cross[j + 1]), fact[j, :, 64:128])
-        parts.append(mixed.astype(BF16))
+    mixed = -dot_high(dot_high(mixed, cross[2]), fact[1, :, 64:128])
+    parts.append(mixed.astype(BF16))
+    parts.append((-dot_high(mixed, cross[1])).astype(BF16))
     gather_core_wait(ITERS)
-
-    def old_rows(b, _):
+    keep_rows = pltpu.make_async_copy(v_row[ITERS], last_rows, out_sem.at[0])
+    keep_rows.start()
+
+    def combine(b, _):
         total = lax.dot_general(parts[0], v_row[2][b], NN, preferred_element_type=F32)
-        for j in (1, 0):
-            total += lax.dot_general(parts[2 - j], v_row[j][b], NN, preferred_element_type=F32)
+        total += lax.dot_general(parts[1], v_row[1][b], NN, preferred_element_type=F32)
+        total += lax.dot_general(parts[2], v_row[0][b], NN, preferred_element_type=F32)
         q_row[b] = total.astype(BF16)
         return 0
 
-    lax.fori_loop(0, 32, old_rows, 0)
-    gram_end(ITERS, True)
+    lax.fori_loop(0, 32, combine, 0, unroll=4)
+    keep_old = pltpu.make_async_copy(q_row, old_rows, out_sem.at[1])
+    keep_old.start()
+    gram_end(ITERS)
     turned = cross[ITERS]
     alphas[ITERS - 1] = turned.T
     betas[ITERS - 1] = fact[ITERS, :, 0:64]
     inverse = fact[ITERS, :, 64:128]
+    factors[0] = inverse
+    factors[1] = -dot_high(inverse, turned)
+    for copy in sent:
+        copy.wait_send()
+    keep_rows.wait()
+    keep_old.wait()
+
+
+def finish(alphas_in, betas_in, factors, last_rows, old_rows, alphas, betas, final):
+    alphas[...] = alphas_in[...]
+    betas[...] = betas_in[...]
+    inverse = factors[0]
     high = inverse.astype(BF16)
     low = (inverse - high.astype(F32)).astype(BF16)
-    back = dot_high(inverse, turned).astype(BF16)
-    for b in range(32):
-        block = v_row[ITERS][b]
-        total = lax.dot_general(high, block, NN, preferred_element_type=F32)
-        total += lax.dot_general(low, block, NN, preferred_element_type=F32)
-        total -= lax.dot_general(back, q_row[b], NN, preferred_element_type=F32)
-        final[:, 256 * b : 256 * b + 256] = total
-    for copy in sent:
-        copy.wait_send()
+    left = jnp.concatenate([high, low, factors[1].astype(BF16)], axis=1)
+    for b in range(last_rows.shape[0]):
+        right = jnp.concatenate([last_rows[b], last_rows[b], old_rows[b]], axis=0)
+        total = lax.dot_general(left, right, NN, preferred_element_type=F32)
+        final[:, 256 * b : 256 * b + 256] = total * math.sqrt(65536)
 
 
 def shards(start_block, tile_values, tile_rows, tile_cols):
     vmem = pl.BlockSpec(memory_space=pltpu.VMEM)
     hbm = pl.BlockSpec(memory_space=pl.ANY)
     dma = pltpu.SemaphoreType.DMA
-    alphas, betas, final = pl.pallas_call(
+    small = jax.ShapeDtypeStruct((ITERS, 64, 64), F32)
+    rows_out = jax.ShapeDtypeStruct((32, 64, 256), BF16)
+    alphas, betas, factors, last_rows, old_rows = pl.pallas_call(
         kernel,
-        out_shape=[
-            jax.ShapeDtypeStruct((ITERS, 64, 64), F32),
-            jax.ShapeDtypeStruct((ITERS, 64, 64), F32),
-            jax.ShapeDtypeStruct((64, 8192), F32),
-        ],
+        out_shape=[small, small, jax.ShapeDtypeStruct((2, 64, 64), F32), rows_out, rows_out],
         in_specs=[vmem, vmem, hbm, hbm],
-        out_specs=[vmem] * 3,
+        out_specs=[vmem, vmem, vmem, hbm, hbm],
         scratch_shapes=[
             pltpu.VMEM((128, 256, 256), BF16),
             pltpu.VMEM((128, 64, 256), F32),
@@ -522,7 +574,7 @@
             pltpu.VMEM((16, 64, 256), F32),
             pltpu.VMEM((16, 64, 256), BF16),
             pltpu.VMEM((16, 64, 256), BF16),
-            pltpu.VMEM((2, 16, 64, 256), BF16),
+            pltpu.VMEM((3, 16, 64, 256), BF16),
             pltpu.VMEM((2, 64, 256), F32),
             pltpu.VMEM((2, 64, 256), F32),
             pltpu.VMEM((128, 512), F32),
@@ -534,28 +586,37 @@
             pltpu.VMEM((4, 64, 64), F32),
             pltpu.VMEM((32, 64, 256), BF16),
             pltpu.VMEM((64, 8192), F32),
+            pltpu.VMEM((64, 4096), F32),
             pltpu.VMEM((8, 32, 128), F32),
             pltpu.VMEM((16, 4, 128), F32),
             pltpu.VMEM((16, 4, 128), F32),
-            pltpu.VMEM((8, 4, 128), F32),
-            pltpu.VMEM((8, 4, 128), F32),
+            pltpu.VMEM((3, 8, 4, 128), F32),
             pltpu.VMEM((16, 4, 128), F32),
             pltpu.VMEM((8, 128), jnp.int32),
             pltpu.VMEM((8, 128), F32),
             pltpu.SMEM((8, 128), jnp.int32),
             pltpu.SMEM((8, 128), F32),
-            dma, dma, dma((2,)),
-            dma, dma, dma((8,)), dma((8,)), dma((8,)), dma((8,)), dma((4,)), dma((4,)),
-            dma((4,)), dma((4,)), dma((8,)), dma((8,)), dma((8,)), dma((2, 8)), dma, dma,
+            dma, dma, dma((2,)), dma((2,)),
+            dma, dma, dma((8,)), dma((8,)),
+            dma, dma((3,)), dma((8,)), dma((8,)), dma((8,)), dma((3, 8)), dma((4,)), dma((4,)),
+            dma((4,)), dma((4,)), dma((8,)), dma((8,)), dma((8,)), dma((3, 8)), dma, dma,
             dma((8,)), dma((8,)),
-            dma((16,)), dma((16,)), dma((8,)), dma((8,)), dma((8,)), dma((8,)), dma((16,)), dma((16,)),
+            dma((16,)), dma((16,)), dma((8,)), dma((3, 8)), dma((16,)), dma((16,)),
         ],
         compiler_params=pltpu.CompilerParams(
             collective_id=0, has_side_effects=True, vmem_limit_bytes=56 * 1024 * 1024
         ),
     )(tile_rows[0], tile_cols[0], start_block, tile_values[0, 0])
-    total_rows = start_block.shape[1] * lax.axis_size("row")
-    return alphas, betas, final * math.sqrt(total_rows)
+    step = 8
+    whole = pl.BlockSpec((ITERS, 64, 64), lambda i: (0, 0, 0))
+    rows = pl.BlockSpec((step, 64, 256), lambda i: (i, 0, 0))
+    return pl.pallas_call(
+        finish,
+        grid=(32 // step,),
+        out_shape=[small, small, jax.ShapeDtypeStruct((64, 8192), F32)],
+        in_specs=[whole, whole, pl.BlockSpec((2, 64, 64), lambda i: (0, 0, 0)), rows, rows],
+        out_specs=[whole, whole, pl.BlockSpec((64, step * 256), lambda i: (0, i))],
+    )(alphas, betas, factors, last_rows, old_rows)
 
 
 def solution(mesh):

time: 187 us -> 157 us (0.84)
  Pallas kernels: 182 us -> 156 us
  other arithmetic: 3.1 us -> 0 us
    pallas_call x1 -> x2, Pallas kernels: 182 us -> 156 us  [the longest x1 152 us: shards(): pl.pallas_call(kernel, out_shape=[small, small, jax.ShapeDtypeStruct((2,...]
    mul x1 -> x0, other arithmetic: 3.1 us -> none  [shards(): return (alphas, betas, final * math.sqrt(total_rows))]
where the time goes in v4:
time: 157 us
  Pallas kernels  156 us (99%)
    pallas_call x1, Pallas kernels, shards(): pl.pallas_call(kernel, out_shape=[small, small, jax.ShapeDtypeStruct((2,...  152 us
    pallas_call x1, Pallas kernels, shards(): pl.pallas_call(finish, grid=(32 // step,), out_shape=[small, small, jax.S...  4.39 us

profile of v4, /device:TPU:1, one launch (start us, length us, event | category | flops | bytes accessed | tf_op | source)
XLA Modules:
  0.0 156.6 jit_solution(1185269687842550700)
XLA Ops:
  0.6 151.6 %shard_map.67 = (f32[3,64,64]{2,1,0:T(8,128)}, f32[3,64,64]{2,1,0:T(8,128)}, f32[2,64,64]{2,1,0:T(8,128)}, bf16[32,64,256]{2,1,0:T(8,128)(2,1)}, bf16[32,64,256]{2,1,0:T(8,128)(2,1)}) custom-call(s32[1,128]{1,0:T(1,128)} %bitcast.4, s32[1,128]{1,0:T(1,128)} %bitcast.5, f32[64,8192]{1,0:T(8,128)} %start.1, bf16[128,256,256]{2,1,0:T(8,128)(2,1)} %bitcast.3), custom_call_target="tpu_custom_call" | custom-call | tf_op jit(solution)/shard_map/pallas_call | solution.py:561
  152.2 4.4 %shard_map.68 = (f32[3,64,64]{2,1,0:T(8,128)}, f32[3,64,64]{2,1,0:T(8,128)}, f32[64,8192]{1,0:T(8,128)}) custom-call(f32[3,64,64]{2,1,0:T(8,128)} %get-tuple-element.8.alphas_in, f32[3,64,64]{2,1,0:T(8,128)} %get-tuple-element.9.betas_in, f32[2,64,64]{2,1,0:T(8,128)} %get-tuple-element.10.factors, bf16[32,64,256]{2,1,0:T(8,128)(2,1)} %get-tuple-element.11.last_rows, ...), custom_call_target="tpu_custom_call" | custom-call | tf_op jit(solution)/shard_map/pallas_call | solution.py:613

commit v5 on v4

--- a/solution.py
+++ b/solution.py
@@ -15,25 +15,52 @@
 NT = (((1,), (1,)), ((), ()))
 NN = (((1,), (0,)), ((), ()))
 UNROLL = 32
-OTHERS = ((0, 2), (0, 1), (0, 3), (1, 0), (1, 2), (1, 1), (1, 3))
+OTHERS = ((0, 1), (0, 3), (1, 0), (0, 2), (1, 1), (1, 3), (1, 2))
 
 
 def dot_high(a, b, dims=NN):
     return lax.dot_general(a, b, dims, precision=HIGH, preferred_element_type=F32)
+
+
+def split(value):
+    high = value.astype(BF16)
+    return high, (value - high.astype(F32)).astype(BF16)
+
+
+def left_terms(value):
+    high, low = split(value)
+    return jnp.concatenate([high, high, low], axis=1)
+
+
+def dot_terms(left, right):
+    high, low = split(right)
+    return lax.dot_general(
+        left, jnp.concatenate([high, low, high], axis=0), NN, preferred_element_type=F32
+    )
 
 
 def factor_rows(rows):
     lane = lax.broadcasted_iota(jnp.int32, (8, 128), 1)
     sub = lax.broadcasted_iota(jnp.int32, (8, 128), 0)
-    for j in range(64):
+    for j in range(0, 64, 2):
         at, inner = divmod(j, 8)
-        pivot_row = rows[at][inner : inner + 1, :]
-        inverse = 1.0 / pivot_row[:, j : j + 1]
+        first = rows[at][inner : inner + 1, :]
+        second = rows[at][inner + 1 : inner + 2, :]
+        left = [jnp.broadcast_to(rows[i][:, j : j + 1], (8, 128)) for i in range(at, 8)]
+        right = [jnp.broadcast_to(rows[i][:, j + 1 : j + 2], (8, 128)) for i in range(at, 8)]
+        a = left[0][inner : inner + 1, :]
+        b = left[0][inner + 1 : inner + 2, :]
+        d = right[0][inner + 1 : inner + 2, :]
+        inverse = 1.0 / (a * d - b * b)
+        over_first = (d * first - b * second) * inverse
+        over_second = (a * second - b * first) * inverse
+        ratio = b * (1.0 / a)
         for i in range(at, 8):
-            scale = jnp.broadcast_to(rows[i][:, j : j + 1] * inverse, (8, 128))
+            change = left[i - at] * over_first + right[i - at] * over_second
             if i == at:
-                scale = jnp.where(sub > inner, scale, 0.0)
-            rows[i] = rows[i] - scale * pivot_row
+                change = jnp.where(sub > inner + 1, change, 0.0)
+                change = jnp.where(sub == inner + 1, ratio * first, change)
+            rows[i] = rows[i] - change
     done = []
     for i in range(8):
         diagonal = jnp.sum(jnp.where(lane == sub + 8 * i, rows[i], 0.0), axis=1, keepdims=True)
@@ -73,7 +100,7 @@
     tiles, slots, v_r0, v_r1, v_r2, v_r3, v_c0, v_c1, v_c2, upper, lower, low_send,
     half_in, x_send, x_in, y_in, col_in, col_sum,
     wq, q_new, applied_old, offset, carried, fact, cross, q_row,
-    start_row, start_col, g_first, g_send, g_one, g_two, g_three,
+    start_row, start_own, start_col, g_first, g_send, g_one, g_two, g_three,
     order_i, order_f, where_i, where_f,
     load_sem, start_sem, order_sem, out_sem,
     sp_s, sp_r, sy_s, sy_r,
@@ -174,7 +201,12 @@
         return remote(g_three.at[p], g_three.at[p], g3_s.at[i], g3_r.at[p], (r, p))
 
     def gram_begin():
-        gram = dot_high(wq[top, :], wq[...], NT)
+        rows = jnp.concatenate(split(wq[top, :]) + split(wq[bottom, :]), axis=0)
+        terms = lax.dot_general(rows[0:128], rows, NT, preferred_element_type=F32)
+        terms = terms[0:64, :] + terms[64:128, :]
+        gram = terms[:, 0:128] + pltpu.roll(terms[:, 0:128], 64, 1)
+        cross_part = terms[:, 128:256] + pltpu.roll(terms[:, 128:256], 64, 1)
+        gram = jnp.where(lax.broadcasted_iota(jnp.int32, (64, 128), 1) < 64, gram, cross_part)
         for i in range(16):
             g_send[i] = gram[4 * i : 4 * i + 4, :]
         each(16, lambda i: one(i).start())
@@ -273,25 +305,22 @@
 
     pl.semaphore_wait(barrier, 24)
     lanes = lambda spot: pl.ds(pl.multiple_of(spot * 256, 512), 512)
-    raw_sent = [
-        remote(
-            start_row.at[:, lanes(home)], start_col.at[:, lanes(4 * x + 2 * zl)], sp_s, sp_r, holder
-        )
-    ]
+    own = start_row[:, lanes(home)]
+    start_own[0] = own[:, 0:256]
+    start_own[1] = own[:, 256:512]
+    raw_sent = [remote(start_own, start_col.at[pl.ds(4 * x + 2 * zl, 2)], sp_s, sp_r, holder)]
     raw_sent[0].start()
 
     def start_gram(i, acc):
         block = start_row[:, pl.ds(pl.multiple_of(i * 512, 512), 512)]
         high = block.astype(BF16)
-        rest = block - high.astype(F32)
-        middle = rest.astype(BF16)
-        low = (rest - middle.astype(F32)).astype(BF16)
-        terms = jnp.concatenate([high, middle, low], axis=0)
+        low = (block - high.astype(F32)).astype(BF16)
+        terms = jnp.concatenate([high, low], axis=0)
         return acc + lax.dot_general(terms, terms, NT, preferred_element_type=F32)
 
-    gram = lax.fori_loop(0, 16, start_gram, jnp.zeros((192, 192), F32))
-    gram = gram[0:64, :] + gram[64:128, :] + gram[128:192, :]
-    gram = gram[:, 0:64] + gram[:, 64:128] + gram[:, 128:192]
+    gram = lax.fori_loop(0, 16, start_gram, jnp.zeros((128, 128), F32), unroll=4)
+    gram = gram[0:64, :] + gram[64:128, :]
+    gram = gram[:, 0:64] + gram[:, 64:128]
     g_first[r, :, 0:64] = gram[0:32, :]
     g_first[r, :, 64:128] = gram[32:64, :]
 
@@ -320,7 +349,7 @@
     ]
     for copy in orders:
         copy.start()
-    chunk = start_col.at[:, lanes(y_spot(0, 0))]
+    chunk = start_col.at[pl.ds(y_spot(0, 0), 2)]
     remote(chunk, chunk, sp_s, sp_r, owner).wait_recv()
     for a, i in OTHERS:
         copy = remote(chunk, chunk, sy_s.at[slot(a, i)], sy_r.at[slot_there(a, i)], y_device(a, i))
@@ -333,28 +362,23 @@
     factorize(0)
     inverse = fact[0, :, 64:128]
     wq[top, :] = dot_high(inverse, start_row[:, lanes(home)])
-    high = inverse.astype(BF16)
-    low = (inverse - high.astype(F32)).astype(BF16)
-    left = jnp.concatenate([high, high, low], axis=1)
+    left = left_terms(inverse)
 
     def solve(source, target, count):
         def step(b, _):
-            block = source[:, pl.ds(pl.multiple_of(b * 256, 256), 256)]
-            upper_half = block.astype(BF16)
-            lower_half = (block - upper_half.astype(F32)).astype(BF16)
-            right = jnp.concatenate([upper_half, lower_half, upper_half], axis=0)
-            target[b] = lax.dot_general(left, right, NN, preferred_element_type=F32).astype(BF16)
+            target[b] = dot_terms(left, source(b)).astype(BF16)
             return 0
 
         lax.fori_loop(0, count, step, 0, unroll=4)
 
-    solve(start_row, v_row[0], 32)
+    solve(lambda b: start_row[:, pl.ds(pl.multiple_of(b * 256, 256), 256)], v_row[0], 32)
     for copy in orders:
         copy.wait()
     each(8, lambda i: zero_out(i).wait_send())
 
-    def iterate(at):
+    def iterate(at, pending):
         sent = []
+        reduced = []
         if at == 0:
             load.wait()
         else:
@@ -365,6 +389,8 @@
             sent += gather_rows_begin(at)
             for copy in sent:
                 copy.start()
+            for copy in pending:
+                copy.wait_send()
             gram_begin()
             part = v_col[at].at[pl.ds(y_spot(0, 0), 2)]
             remote(part, part, agp_s, agp_r.at[at], owner).wait_recv()
@@ -394,14 +420,14 @@
                 rsy_s.at[slot(a, i)], rsy_r.at[at, slot_there(a, i)], y_device(a, i),
             )
             copy.start()
-            sent.append(copy)
+            reduced.append(copy)
         if at == 0:
             for a, i in OTHERS:
-                part = start_col.at[:, lanes(y_spot(a, i))]
+                part = start_col.at[pl.ds(y_spot(a, i), 2)]
                 remote(
                     part, part, sy_s.at[slot(a, i)], sy_r.at[slot(a, i)], y_device(a, i)
                 ).wait_recv()
-            solve(start_col, v_col[0], 16)
+            solve(lambda b: start_col[b], v_col[0], 16)
         else:
             gram_third(at - 1)
             for a, i in OTHERS:
@@ -422,7 +448,7 @@
                 rsc_s.at[i], rsc_r.at[i], core,
             )
             copy.start()
-            sent.append(copy)
+            reduced.append(copy)
         for i in (2, 1, 3, 0):
             q = x_at[i]
             theirs = half_in.at[pl.ds(4 * q, 4)]
@@ -443,7 +469,7 @@
                         rsx_s.at[slot(a, i)], rsx_r.at[slot_there(a, i)], x_device(a, i),
                     )
                     copy.start()
-                    sent.append(copy)
+                    reduced.append(copy)
         for a, i in OTHERS:
             part = y_in.at[at, pl.ds(2 * slot(a, i), 2)]
             remote(
@@ -456,13 +482,14 @@
             col_sum[b] = total
         copy = remote(col_sum, col_in, rsp_s, rsp_r, owner)
         copy.start()
-        sent.append(copy)
+        reduced.append(copy)
         if at == 0:
             wq[bottom, :] = wq[top, :]
         else:
             gram_end(at)
             turned = cross[at]
             inverse = fact[at, :, 64:128]
+            terms = left_terms(inverse)
             old = wq[bottom, :]
             q_new[...] = dot_high(inverse, wq[top, :] - dot_high(turned, old))
             offset[...] = dot_high(inverse, dot_high(turned, applied_old[...]))
@@ -488,14 +515,16 @@
                 applied_old[:, spot] = product
                 wq[top, spot] = product
             else:
-                applied = dot_high(inverse, product) - offset[:, spot]
+                applied = dot_terms(terms, product) - offset[:, spot]
                 applied_old[:, spot] = applied
                 wq[top, spot] = applied - carried[:, spot]
         for copy in sent:
             copy.wait_send()
-
+        return reduced
+
+    pending = []
     for at in range(ITERS):
-        iterate(at)
+        pending = iterate(at, pending)
     for copy in raw_sent:
         copy.wait_send()
 
@@ -504,6 +533,8 @@
     gram_begin()
     for copy in sent:
         copy.start()
+    for copy in pending:
+        copy.wait_send()
     gram_second(ITERS - 1)
     sent += gather_rows_finish(ITERS)
     gram_third(ITERS - 1)
@@ -586,7 +617,8 @@
             pltpu.VMEM((4, 64, 64), F32),
             pltpu.VMEM((32, 64, 256), BF16),
             pltpu.VMEM((64, 8192), F32),
-            pltpu.VMEM((64, 4096), F32),
+            pltpu.VMEM((2, 64, 256), F32),
+            pltpu.VMEM((16, 64, 256), F32),
             pltpu.VMEM((8, 32, 128), F32),
             pltpu.VMEM((16, 4, 128), F32),
             pltpu.VMEM((16, 4, 128), F32),
@@ -607,7 +639,7 @@
             collective_id=0, has_side_effects=True, vmem_limit_bytes=56 * 1024 * 1024
         ),
     )(tile_rows[0], tile_cols[0], start_block, tile_values[0, 0])
-    step = 8
+    step = 16
     whole = pl.BlockSpec((ITERS, 64, 64), lambda i: (0, 0, 0))
     rows = pl.BlockSpec((step, 64, 256), lambda i: (i, 0, 0))
     return pl.pallas_call(

time: 157 us -> 151 us (0.962)
  Pallas kernels: 156 us -> 151 us
    pallas_call x1, Pallas kernels: 152 us -> 147 us  [shards(): pl.pallas_call(kernel, out_shape=[small, small, jax.ShapeDtypeStruct((2,...]
where the time goes in v5:
time: 151 us
  Pallas kernels  151 us (100%)
    pallas_call x1, Pallas kernels, shards(): pl.pallas_call(kernel, out_shape=[small, small, jax.ShapeDtypeStruct((2,...  147 us
    pallas_call x1, Pallas kernels, shards(): pl.pallas_call(finish, grid=(32 // step,), out_shape=[small, small, jax.S...  3.18 us

profile of v5, /device:TPU:1, one launch (start us, length us, event | category | flops | bytes accessed | tf_op | source)
XLA Modules:
  0.0 151.3 jit_solution(12101422704887207648)
XLA Ops:
  0.6 147.5 %shard_map.67 = (f32[3,64,64]{2,1,0:T(8,128)}, f32[3,64,64]{2,1,0:T(8,128)}, f32[2,64,64]{2,1,0:T(8,128)}, bf16[32,64,256]{2,1,0:T(8,128)(2,1)}, bf16[32,64,256]{2,1,0:T(8,128)(2,1)}) custom-call(s32[1,128]{1,0:T(1,128)} %bitcast.4, s32[1,128]{1,0:T(1,128)} %bitcast.5, f32[64,8192]{1,0:T(8,128)} %start.1, bf16[128,256,256]{2,1,0:T(8,128)(2,1)} %bitcast.3), custom_call_target="tpu_custom_call" | custom-call | tf_op jit(solution)/shard_map/pallas_call | solution.py:592
  148.1 3.2 %shard_map.68 = (f32[3,64,64]{2,1,0:T(8,128)}, f32[3,64,64]{2,1,0:T(8,128)}, f32[64,8192]{1,0:T(8,128)}) custom-call(f32[3,64,64]{2,1,0:T(8,128)} %get-tuple-element.8.alphas_in, f32[3,64,64]{2,1,0:T(8,128)} %get-tuple-element.9.betas_in, f32[2,64,64]{2,1,0:T(8,128)} %get-tuple-element.10.factors, bf16[32,64,256]{2,1,0:T(8,128)(2,1)} %get-tuple-element.11.last_rows, ...), custom_call_target="tpu_custom_call" | custom-call | tf_op jit(solution)/shard_map/pallas_call | solution.py:645

commit v6 on v5

--- a/solution.py
+++ b/solution.py
@@ -251,14 +251,26 @@
         block = v_row[at].at[pl.ds(home, 2)]
         return [
             remote(block, block, agx_s.at[slot(a, i)], agx_r.at[slot_there(a, i)], x_device(a, i))
-            for a, i in OTHERS
+            for a, i in ((1, 0), (0, 1), (0, 3), (0, 2))
         ]
+
+    def gather_rows_forward(at):
+        block = v_row[at].at[pl.ds(mine + x_spot(1, 0), 2)]
+        s, d = agx_s.at[slot(1, 0)], agx_r.at[slot(1, 0)]
+        remote(block, block, s, d, x_device(1, 0)).wait_recv()
+        sent = [
+            remote(block, block, agx_s.at[slot(1, i)], agx_r.at[slot_there(1, i)], x_device(0, i))
+            for i in (1, 3, 2)
+        ]
+        for copy in sent:
+            copy.start()
+        return sent
 
     def gather_rows_finish(at):
         sent = []
         for i in (0, 1, 3, 2):
             for a in (0, 1):
-                if (a, i) != (0, 0):
+                if i > 0:
                     block = v_row[at].at[pl.ds(mine + x_spot(a, i), 2)]
                     remote(
                         block, block, agx_s.at[slot(a, i)], agx_r.at[slot(a, i)], x_device(a, i)
@@ -351,11 +363,17 @@
         copy.start()
     chunk = start_col.at[pl.ds(y_spot(0, 0), 2)]
     remote(chunk, chunk, sp_s, sp_r, owner).wait_recv()
-    for a, i in OTHERS:
+    for a, i in ((1, 0), (0, 1), (0, 3), (0, 2)):
         copy = remote(chunk, chunk, sy_s.at[slot(a, i)], sy_r.at[slot_there(a, i)], y_device(a, i))
         copy.start()
         raw_sent.append(copy)
     each(8, lambda i: zero_in(i).wait_recv())
+    chunk = start_col.at[pl.ds(y_spot(1, 0), 2)]
+    remote(chunk, chunk, sy_s.at[slot(1, 0)], sy_r.at[slot(1, 0)], y_device(1, 0)).wait_recv()
+    for i in (1, 3, 2):
+        copy = remote(chunk, chunk, sy_s.at[slot(1, i)], sy_r.at[slot_there(1, i)], y_device(0, i))
+        copy.start()
+        raw_sent.append(copy)
     total = jnp.sum(g_first[...], axis=0)
     fact[0, 0:32, 0:64] = total[:, 0:64]
     fact[0, 32:64, 0:64] = total[:, 64:128]
@@ -392,6 +410,7 @@
             for copy in pending:
                 copy.wait_send()
             gram_begin()
+            sent += gather_rows_forward(at)
             part = v_col[at].at[pl.ds(y_spot(0, 0), 2)]
             remote(part, part, agp_s, agp_r.at[at], owner).wait_recv()
             for a, i in OTHERS:
@@ -422,7 +441,7 @@
             copy.start()
             reduced.append(copy)
         if at == 0:
-            for a, i in OTHERS:
+            for a, i in ((0, 1), (0, 3), (0, 2), (1, 1), (1, 3), (1, 2)):
                 part = start_col.at[pl.ds(y_spot(a, i), 2)]
                 remote(
                     part, part, sy_s.at[slot(a, i)], sy_r.at[slot(a, i)], y_device(a, i)
@@ -535,6 +554,7 @@
         copy.start()
     for copy in pending:
         copy.wait_send()
+    sent += gather_rows_forward(ITERS)
     gram_second(ITERS - 1)
     sent += gather_rows_finish(ITERS)
     gram_third(ITERS - 1)

time: 151 us -> 144 us (0.954)
  Pallas kernels: 151 us -> 143 us
    pallas_call x1, Pallas kernels: 147 us -> 139 us  [shards(): pl.pallas_call(kernel, out_shape=[small, small, jax.ShapeDtypeStruct((2,...]
where the time goes in v6:
time: 144 us; the launch traced here: 143 us
  Pallas kernels  143 us (99%)
    pallas_call x1, Pallas kernels, shards(): pl.pallas_call(kernel, out_shape=[small, small, jax.ShapeDtypeStruct((2,...  139 us
    pallas_call x1, Pallas kernels, shards(): pl.pallas_call(finish, grid=(32 // step,), out_shape=[small, small, jax.S...  3.18 us

profile of v6, /device:TPU:1, one launch (start us, length us, event | category | flops | bytes accessed | tf_op | source)
XLA Modules:
  0.0 143.2 jit_solution(3556605174636279614)
XLA Ops:
  0.6 139.4 %shard_map.67 = (f32[3,64,64]{2,1,0:T(8,128)}, f32[3,64,64]{2,1,0:T(8,128)}, f32[2,64,64]{2,1,0:T(8,128)}, bf16[32,64,256]{2,1,0:T(8,128)(2,1)}, bf16[32,64,256]{2,1,0:T(8,128)(2,1)}) custom-call(s32[1,128]{1,0:T(1,128)} %bitcast.4, s32[1,128]{1,0:T(1,128)} %bitcast.5, f32[64,8192]{1,0:T(8,128)} %start.1, bf16[128,256,256]{2,1,0:T(8,128)(2,1)} %bitcast.3), custom_call_target="tpu_custom_call" | custom-call | tf_op jit(solution)/shard_map/pallas_call | solution.py:612
  140.0 3.2 %shard_map.68 = (f32[3,64,64]{2,1,0:T(8,128)}, f32[3,64,64]{2,1,0:T(8,128)}, f32[64,8192]{1,0:T(8,128)}) custom-call(f32[3,64,64]{2,1,0:T(8,128)} %get-tuple-element.8.alphas_in, f32[3,64,64]{2,1,0:T(8,128)} %get-tuple-element.9.betas_in, f32[2,64,64]{2,1,0:T(8,128)} %get-tuple-element.10.factors, bf16[32,64,256]{2,1,0:T(8,128)(2,1)} %get-tuple-element.11.last_rows, ...), custom_call_target="tpu_custom_call" | custom-call | tf_op jit(solution)/shard_map/pallas_call | solution.py:665
